TPU v7x, 32 devices: a whole 2x2x4 slice. The times are simulated.
32 devices in a mesh: dp: 2 (over x), width: 4 (over y, core), hidden: 4 (over z).
Axes of the slice: x: 2, y: 2, z: 4, core: 2. Of those that a mesh axis runs over, the one named last changes fastest.
Arguments:
- tokens: bfloat16 [1024, 8192], P('dp', 'width'), may hold values from -6 to 6
- target: bfloat16 [1024, 8192], P('dp', 'width'), may hold values from -6 to 6
- gate_weight: bfloat16 [8192, 14336], P('width', 'hidden'), may hold values from -0.0625 to 0.0625
- up_weight: bfloat16 [8192, 14336], P('width', 'hidden'), may hold values from -0.0625 to 0.0625
- down_weight: bfloat16 [14336, 8192], P('hidden', 'width'), may hold values from -0.046875 to 0.046875
- probe_sign: bfloat16 [8192, 14336], P('width', 'hidden'), may hold values from -1 to 1, as said below
Outputs:
- gate_grad: bfloat16 [8192, 14336], P(('width', 'dp'), 'hidden')
- hess_diag: bfloat16 [8192, 14336], P(('width', 'dp'), 'hidden')
Inputs may be any that keep to these rules, and one draw needn't show every extreme that they name: `probe_sign`: every entry is -1 or +1.
All inputs are finite; a program needn't handle non-finite values.
Results may differ from a plain program's by a relative error of at most 0.019.
Values may be sent and summed in bfloat16 or wider, within the bound.
A program may use at most 192 MiB of HBM per device.

v0:
```python
import math

import jax
import jax.numpy as jnp
from jax import lax
from jax.sharding import PartitionSpec as P

D = 8192


def matmul(left, right):
    return jnp.dot(left, right, preferred_element_type=jnp.float32)


def right_trans(left, right):
    return lax.dot_general(
        left, right, (((1,), (1,)), ((), ())), preferred_element_type=jnp.float32
    )


def left_trans(left, right):
    return lax.dot_general(
        left, right, (((0,), (0,)), ((), ())), preferred_element_type=jnp.float32
    )


def coefficients(gate_pre, up_pre, tangent):
    sigmoid_gate = jax.nn.sigmoid(gate_pre)
    first = sigmoid_gate * (1.0 + gate_pre * (1.0 - sigmoid_gate))
    second = sigmoid_gate * (1.0 - sigmoid_gate) * (2.0 + gate_pre * (1.0 - 2.0 * sigmoid_gate))
    hidden = (gate_pre * sigmoid_gate * up_pre).astype(jnp.bfloat16)
    hidden_dot = (first * tangent * up_pre).astype(jnp.bfloat16)
    coeff_first = (first * up_pre).astype(jnp.bfloat16)
    coeff_second = (second * tangent * up_pre).astype(jnp.bfloat16)
    return (hidden, hidden_dot, coeff_first, coeff_second)


def errors(back, back_dot, coeff_first, coeff_second):
    first_f = coeff_first.astype(jnp.float32)
    err_grad = (back * first_f).astype(jnp.bfloat16)
    err_hess = (back * coeff_second.astype(jnp.float32) + back_dot * first_f).astype(jnp.bfloat16)
    return (err_grad, err_hess)


def on_device(tokens, target, gate_weight, up_weight, down_weight, probe_sign):
    inv_width = 1.0 / math.sqrt(D)
    token_rows = tokens.shape[0]
    token_scale = 1.0 / math.sqrt(token_rows * lax.axis_size("dp"))
    gate_pre, up_pre, tangent = lax.psum(
        (
            matmul(tokens, gate_weight),
            matmul(tokens, up_weight),
            matmul(tokens, probe_sign) * inv_width,
        ),
        "width",
    )
    hidden, hidden_dot, coeff_first, coeff_second = coefficients(gate_pre, up_pre, tangent)
    output, output_dot = lax.psum(
        (matmul(hidden, down_weight), matmul(hidden_dot, down_weight)), "hidden"
    )
    resid = (output - target.astype(jnp.float32)).astype(jnp.bfloat16)
    output_dot_b = output_dot.astype(jnp.bfloat16)
    back, back_dot = lax.psum(
        (right_trans(resid, down_weight), right_trans(output_dot_b, down_weight)), "width"
    )
    err_grad, err_hess = errors(back, back_dot, coeff_first, coeff_second)
    grad_term = left_trans(tokens, err_grad) * token_scale
    hess_term = left_trans(tokens, err_hess) * token_scale
    grad_sum, hv_sum = (
        lax.psum_scatter(
            grad_term.astype(jnp.bfloat16), "dp", scatter_dimension=0, tiled=True
        ).astype(jnp.float32),
        lax.psum_scatter(
            hess_term.astype(jnp.bfloat16), "dp", scatter_dimension=0, tiled=True
        ).astype(jnp.float32),
    )
    half_rows = grad_sum.shape[0]
    probe_rows = lax.dynamic_slice_in_dim(
        probe_sign, lax.axis_index("dp") * half_rows, half_rows, 0
    )
    gate_grad = grad_sum.astype(jnp.bfloat16)
    hess_diag = (probe_rows.astype(jnp.float32) * hv_sum * inv_width).astype(jnp.bfloat16)
    return (gate_grad, hess_diag)


def solution(mesh):
    return jax.shard_map(
        on_device,
        mesh=mesh,
        in_specs=(
            P("dp", "width"),
            P("dp", "width"),
            P("width", "hidden"),
            P("width", "hidden"),
            P("hidden", "width"),
            P("width", "hidden"),
        ),
        out_specs=(P(("width", "dp"), "hidden"), P(("width", "dp"), "hidden")),
        check_vma=False,
    )
```

profile of v0, /device:TPU:1, one launch (start us, length us, event | category | flops | bytes accessed | tf_op | source)
XLA Modules:
  0.0 1391.3 jit_solution(12084181178967205965)
XLA Ops:
  7.2 0.0 copy-start
  7.2 0.0 all-reduce.11.cloned.1.call-start
  7.2 1.5 copy-done
  8.8 13.0 convolution_multiply_fusion
  21.7 0.0 copy-done.1
  21.7 9.8 fusion.22
  31.5 12.8 fusion.23
  44.4 0.0 all-reduce.11.cloned.1.call-update
  44.4 0.2 all-reduce.7.cloned.1.call-start
  44.6 375.4 %all-reduce.11.cloned.1.call-done = (f32[512,3584]{1,0:T(8,128)}, f32[512,3584]{1,0:T(8,128)}, f32[512,3584]{1,0:T(8,128)}) async-done(((f32[512,3584]{1,0:T(8,128)}, f32[512,3584]{1,0:T(8,128)}, f32[512,3584]{1,0:T(8,128)}), (f32[512,3584]{1,0:T(8,128)}, f32[512,3584]{1,0:T(8,128)}, f32[512,3584]{1,0:T(8,128)})) %all-reduce.11.cloned.1.call-update) | async-done | bytes 22020112 | tf_op jit(solution)/shard_map/psum | solution.py:49
  420.0 16.7 %fusion.13 = f32[512,2048]{1,0:T(8,128)} fusion(bf16[3584,2048]{1,0:T(8,128)(2,1)} %param.10, f32[512,3584]{1,0:T(8,128)} %get-tuple-element.6, f32[512,3584]{1,0:T(8,128)} %get-tuple-element.7), kind=kOutput, calls=%fused_computation.25 | convolution fusion | flops 7527202816 | bytes 33554432 | tf_op jit(solution)/shard_map/dot_general | solution.py:12
  436.6 21.6 %fusion.11 = f32[512,2048]{1,0:T(8,128)} fusion(bf16[3584,2048]{1,0:T(8,128)(2,1)} %param.10, f32[512,3584]{1,0:T(8,128)} %get-tuple-element.6, f32[512,3584]{1,0:T(8,128)} %get-tuple-element.8, f32[512,3584]{1,0:T(8,128)} %get-tuple-element.7), kind=kOutput, calls=%fused_computation.24 | convolution fusion | flops 7534542848 | bytes 40894464 | tf_op jit(solution)/shard_map/dot_general | solution.py:12
  458.2 0.0 all-reduce.7.cloned.1.call-update
  458.2 0.0 all-reduce.9.cloned.1.call-start
  458.3 269.6 %all-reduce.12 = bf16[512,2048]{1,0:T(8,128)(2,1)} all-reduce(f32[512,2048]{1,0:T(8,128)} %fusion.11), channel_id=1, replica_groups=mesh['dp'=2,'width'=4,'hidden'=4] {'hidden'}, use_global_device_ids=true, to_apply=%region_6.0 | all-reduce | flops 1048576 | bytes 6291456 | tf_op jit(solution)/shard_map/psum | solution.py:58
  727.9 13.5 fusion.24
  741.4 14.7 %fusion.15 = f32[512,3584]{1,0:T(8,128)} fusion(bf16[3584,2048]{1,0:T(8,128)(2,1)} %param.10, f32[512,2048]{1,0:T(8,128)} %all-reduce.7.cloned.1.call-done, bf16[512,2048]{1,0:T(8,128)(2,1)} %param.7), kind=kOutput, calls=%fused_computation.26 | convolution fusion | flops 7519338496 | bytes 28311552 | tf_op jit(solution)/shard_map/dot_general | solution.py:16
  756.1 0.0 all-reduce.9.cloned.1.call-update
  756.1 0.0 reduce-scatter.5.cloned.1.call-start
  756.2 260.0 %all-reduce.9.cloned.1.call-done = (f32[512,3584]{1,0:T(8,128)}, f32[512,3584]{1,0:T(8,128)}) async-done(((f32[512,3584]{1,0:T(8,128)}, f32[512,3584]{1,0:T(8,128)}), (f32[512,3584]{1,0:T(8,128)}, f32[512,3584]{1,0:T(8,128)})) %all-reduce.9.cloned.1.call-update) | async-done | bytes 14680080 | tf_op jit(solution)/shard_map/psum | solution.py:63
  1016.2 21.3 %fusion.1 = bf16[2048,3584]{0,1:T(8,128)(2,1)} fusion(bf16[512,2048]{1,0:T(8,128)(2,1)S(1)} %copy-done, f32[512,3584]{1,0:T(8,128)} %get-tuple-element.5, f32[512,3584]{1,0:T(8,128)} %get-tuple-element.4, f32[512,3584]{1,0:T(8,128)} %get-tuple-element.6, f32[512,3584]{1,0:T(8,128)} %get-tuple-element.8, f32[512,3584]{1,0:T(8,128)} %get-tuple-element.7), kind=kOutput, calls=%fused_computation.4 | convolution fusion | flops 7574913024 | bytes 53477376 | tf_op jit(solution)/shard_map/dot_general | solution.py:22
  1037.4 0.0 reduce-scatter.5.cloned.1.call-update
  1037.4 0.3 reduce-scatter.3.cloned.1.call-start
  1037.7 23.5 %fusion = bf16[2048,3584]{0,1:T(8,128)(2,1)} fusion(bf16[512,2048]{1,0:T(8,128)(2,1)S(1)} %copy-done, f32[512,3584]{1,0:T(8,128)} %get-tuple-element.4, f32[512,3584]{1,0:T(8,128)} %get-tuple-element.6, f32[512,3584]{1,0:T(8,128)} %get-tuple-element.7), kind=kOutput, calls=%fused_computation.3 | convolution fusion | flops 7552892928 | bytes 38797312 | tf_op jit(solution)/shard_map/dot_general | solution.py:22
  1061.3 0.0 reduce-scatter.3.cloned.1.call-update
  1061.3 6.6 constant_dynamic-slice_fusion
  1067.9 10.4 copy.11
  1078.3 126.9 %reduce-scatter.5.cloned.1.call-done = bf16[1024,3584]{0,1:T(8,128)(2,1)} async-done(((bf16[2048,3584]{0,1:T(8,128)(2,1)}), bf16[1024,3584]{0,1:T(8,128)(2,1)}) %reduce-scatter.5.cloned.1.call-update) | async-done | bytes 7340048 | tf_op jit(solution)/shard_map/reduce_scatter | solution.py:73
  1205.2 12.0 multiply_convert_fusion.2
  1217.2 9.9 copy.10
  1227.1 147.3 %reduce-scatter.3.cloned.1.call-done = bf16[1024,3584]{0,1:T(8,128)(2,1)} async-done(((bf16[2048,3584]{0,1:T(8,128)(2,1)}), bf16[1024,3584]{0,1:T(8,128)(2,1)}) %reduce-scatter.3.cloned.1.call-update) | async-done | bytes 7340048 | tf_op jit(solution)/shard_map/reduce_scatter | solution.py:70
  1374.4 9.9 copy.9
  (2 shorter events, 0.0 us)
Async XLA Ops:
  7.2 1.6 copy-start
  7.2 412.8 %all-reduce.11.cloned.1.call-start = ((), (), s32[]{:S(2)}) async-start(), calls=%async_computation.6 | async-start | bytes 44040192 | tf_op jit(solution)/shard_map/psum | solution.py:49
  8.8 13.0 copy-start.1
  44.4 697.0 %all-reduce.7.cloned.1.call-start = ((), (), s32[]{:S(2)}) async-start(), calls=%async_computation.2 | async-start | bytes 8388608 | tf_op jit(solution)/shard_map/psum | solution.py:58
  458.2 557.9 %all-reduce.9.cloned.1.call-start = ((), (), s32[]{:S(2)}) async-start(), calls=%async_computation.5 | async-start | bytes 29360128 | tf_op jit(solution)/shard_map/psum | solution.py:63
  756.1 449.0 %reduce-scatter.5.cloned.1.call-start = ((), (), s32[]{:S(2)}) async-start(), calls=%async_computation.4 | async-start | bytes 22020096 | tf_op jit(solution)/shard_map/reduce_scatter | solution.py:73
  1037.4 337.0 %reduce-scatter.3.cloned.1.call-start = ((), (), s32[]{:S(2)}) async-start(), calls=%async_computation.3 | async-start | bytes 22020096 | tf_op jit(solution)/shard_map/reduce_scatter | solution.py:70
Sparse Core Ops, SparseCore 0:
  44.5 375.4 all-reduce.10
  458.3 278.1 all-reduce.6
  756.3 259.8 all-reduce.8
  1037.6 167.5 reduce-scatter.4
  1207.3 167.0 reduce-scatter.2
where the time goes:
time: 1400 us; the launch traced here: 1390 us
  waiting for transfers between devices  910 us (65%)
  blocking collectives  270 us (19%)
  matrix products  147 us (10%)
  local copies, waits for them, and re-layouts  38.4 us (3%)
  between operations  14.2 us (1%)
    psum x1, waiting for transfers between devices, on_device(): lax.psum((matmul(tokens, gate_weight), matmul(tokens, up_weight), matmul(...  375 us
    psum x1, blocking collectives, on_device(): lax.psum((matmul(hidden, down_weight), matmul(hidden_dot, down_weight)),...  270 us
    psum x1, waiting for transfers between devices, on_device(): lax.psum((right_trans(resid, down_weight), right_trans(output_dot_b, down...  260 us
    reduce_scatter x1, waiting for transfers between devices, on_device(): lax.psum_scatter(grad_term.astype(jnp.bfloat16), 'dp', scatter_dimension=...  147 us
    reduce_scatter x1, waiting for transfers between devices, on_device(): lax.psum_scatter(hess_term.astype(jnp.bfloat16), 'dp', scatter_dimension=...  127 us
    dot_general x5, matrix products, matmul(): return jnp.dot(left, right, preferred_element_type=jnp.float32)  73.8 us
    dot_general x2, matrix products, left_trans(): lax.dot_general(left, right, (((0,), (0,)), ((), ())), preferred_element_...  44.8 us
    unnamed x7, local copies, waits for them, and re-layouts  31.8 us
  transfers between devices with their start and end apart: 5, of which 4 were waited for; matrix products, arithmetic and copies ran while one was open for 5% of the time, Pallas kernels for 0%

commit v1 on v0

v1 whole, which is shorter than its diff:
```python
import math

import jax
import jax.numpy as jnp
from jax import lax
from jax.sharding import PartitionSpec as P

D = 8192
CHUNKS = 2
BF16 = jnp.bfloat16
F32 = jnp.float32


def matmul(left, right, dims=((1,), (0,)), out=BF16):
    return lax.dot_general(left, right, (dims, ((), ())), preferred_element_type=F32).astype(out)


def shift_core(x):
    n = lax.axis_size("width")
    return lax.ppermute(x, "width", [(i, i ^ 1) for i in range(n)])


def shift_y(x):
    n = lax.axis_size("width")
    return lax.ppermute(x, "width", [(i, (i + 2) % n) for i in range(n)])


def shift_z(x, step):
    n = lax.axis_size("hidden")
    return lax.ppermute(x, "hidden", [(i, (i + step) % n) for i in range(n)])


def shift_dp(x):
    n = lax.axis_size("dp")
    return lax.ppermute(x, "dp", [(i, (i + 1) % n) for i in range(n)])


def add(left, right):
    return left.astype(F32) + right.astype(F32)


def reduce_width(x):
    ny = x.shape[0]
    x = add(x[:, 0], shift_core(x[:, 1]))
    total = x[ny - 1]
    for step in range(ny - 1):
        total = add(x[ny - 2 - step], shift_y(total.astype(BF16)))
    return total


def gather_width(x, ny):
    pieces = [None] * ny
    pieces[0] = x
    for step in range(ny - 1):
        x = shift_y(x)
        pieces[ny - 1 - step] = x
    return pieces


def reduce_hidden(x, step):
    n = len(x)
    at = (-step) % n
    total = x[at]
    for _ in range(n - 1):
        at = (at - step) % n
        total = add(x[at], shift_z(total.astype(BF16), step))
    return total


def gather_hidden(x, step, n):
    pieces = [None] * n
    pieces[0] = x
    at = 0
    for _ in range(n - 1):
        at = (at - step) % n
        x = shift_z(x, step)
        pieces[at] = x
    return pieces


def coefficients(gate_pre, up_pre, tangent):
    sigmoid_gate = jax.nn.sigmoid(gate_pre)
    first = sigmoid_gate * (1.0 + gate_pre * (1.0 - sigmoid_gate))
    second = sigmoid_gate * (1.0 - sigmoid_gate) * (2.0 + gate_pre * (1.0 - 2.0 * sigmoid_gate))
    hidden = (gate_pre * sigmoid_gate * up_pre).astype(BF16)
    hidden_dot = (first * tangent * up_pre).astype(BF16)
    coeff_first = (first * up_pre).astype(BF16)
    coeff_second = (second * tangent * up_pre).astype(BF16)
    return (hidden, hidden_dot, coeff_first, coeff_second)


def errors(back, back_dot, coeff_first, coeff_second):
    first_f = coeff_first.astype(F32)
    err_grad = (back * first_f).astype(BF16)
    err_hess = (back * coeff_second.astype(F32) + back_dot * first_f).astype(BF16)
    return (err_grad, err_hess)


def on_device(tokens, target, gate_weight, up_weight, down_weight, probe_sign):
    inv_width = 1.0 / math.sqrt(D)
    n_dp = lax.axis_size("dp")
    n_width = lax.axis_size("width")
    nz = lax.axis_size("hidden")
    ny = n_width // 2
    rows, cols = tokens.shape
    ff = gate_weight.shape[1]
    token_scale = 1.0 / math.sqrt(rows * n_dp)
    half = cols // n_dp
    t = rows // CHUNKS
    r = t // (n_width * nz)
    dp = lax.axis_index("dp")
    w = lax.axis_index("width")
    z = lax.axis_index("hidden")

    row = lax.broadcasted_iota(jnp.int32, (rows, rows), 0)
    col = lax.broadcasted_iota(jnp.int32, (rows, rows), 1)
    sz = (row // r) % nz
    pc = (row // (r * nz)) % 2
    py = (row // (r * nz * 2)) % ny
    source = (
        (row // t) * t
        + ((((py + w // 2) % ny) * 2 + (pc + w % 2) % 2) * nz + (sz + z) % nz) * r
        + row % r
    )
    order = (source == col).astype(BF16)
    tokens = matmul(order, tokens)
    target = matmul(order, target)
    mine = lax.dynamic_slice_in_dim(tokens, dp * half, half, 1)
    other = shift_dp(lax.dynamic_slice_in_dim(tokens, (1 - dp) * half, half, 1))

    def stage_a(k):
        tok = tokens[k * t:(k + 1) * t]
        pre = [
            reduce_width(matmul(tok, weight).reshape(ny, 2, nz * r, ff))
            for weight in (gate_weight, up_weight, probe_sign)
        ]
        hidden, hidden_dot, c1, c2 = coefficients(pre[0], pre[1], pre[2] * inv_width)
        both = jnp.stack([hidden, hidden_dot])
        own = jnp.stack(gather_width(both, ny), axis=1)
        full = jnp.stack([own, shift_core(own)], axis=2)
        return full.reshape(2 * t, ff), c1, c2

    def stage_b(k, full):
        out = matmul(full, down_weight).reshape(2, n_width, nz, r, cols)
        result = []
        for i, step in ((0, 1), (1, -1)):
            total = reduce_hidden([out[i, :, s] for s in range(nz)], step)
            if i == 0:
                goal = target[k * t:(k + 1) * t].reshape(n_width, nz, r, cols)[:, 0]
                total = total - goal.astype(F32)
            pieces = gather_hidden(total.astype(BF16), step, nz)
            result.append(jnp.stack(pieces, axis=1).reshape(t, cols))
        return result

    def stage_c(resid, output_dot, c1, c2):
        back, back_dot = [
            reduce_width(matmul(v, down_weight, ((1,), (1,))).reshape(ny, 2, nz * r, ff))
            for v in (resid, output_dot)
        ]
        result = []
        for err in errors(back, back_dot, c1, c2):
            own = gather_width(err, ny)
            far = [shift_dp(piece) for piece in own]
            part = jnp.stack(own + far)
            result.append(jnp.stack([part, shift_core(part)], axis=1).reshape(n_dp * t, ff))
        return result

    a = [stage_a(k) for k in range(CHUNKS)]
    b = [stage_b(k, a[k][0]) for k in range(CHUNKS)]
    c = [stage_c(*b[k], a[k][1], a[k][2]) for k in range(CHUNKS)]
    sums = [None, None]
    for k in range(CHUNKS):
        tok = jnp.concatenate([mine[k * t:(k + 1) * t], other[k * t:(k + 1) * t]])
        for i in range(2):
            term = matmul(tok, c[k][i], ((0,), (0,)), F32)
            sums[i] = term if sums[i] is None else sums[i] + term
    probe_rows = lax.dynamic_slice_in_dim(probe_sign, dp * half, half, 0)
    gate_grad = (sums[0] * token_scale).astype(BF16)
    hess_diag = (probe_rows.astype(F32) * (sums[1] * token_scale) * inv_width).astype(BF16)
    return (gate_grad, hess_diag)


def solution(mesh):
    return jax.shard_map(
        on_device,
        mesh=mesh,
        in_specs=(
            P("dp", "width"),
            P("dp", "width"),
            P("width", "hidden"),
            P("width", "hidden"),
            P("hidden", "width"),
            P("width", "hidden"),
        ),
        out_specs=(P(("width", "dp"), "hidden"), P(("width", "dp"), "hidden")),
        check_vma=False,
    )
```

time: 1400 us -> 553 us (0.40)
  waiting for transfers between devices: 910 us -> 242 us
  blocking collectives: 270 us -> 0 us
  starting transfers between devices: 0.63 us -> 66 us
  matrix products: 147 us -> 175 us
  other arithmetic: 12 us -> 28 us
    psum x3 -> x0, waiting for transfers between devices: 635 us -> none  [the longest x1 375 us: on_device(): lax.psum((matmul(tokens, gate_weight), matmul(tokens, up_weight), matmul(...]
    reduce_scatter x2 -> x0, waiting for transfers between devices: 274 us -> none  [the longest x1 147 us: on_device(): lax.psum_scatter(grad_term.astype(jnp.bfloat16), 'dp', scatter_dimension=...]
    psum x1 -> x0, blocking collectives: 270 us -> none  [on_device(): lax.psum((matmul(hidden, down_weight), matmul(hidden_dot, down_weight)),...]
    ppermute x0 -> x65, waiting for transfers between devices: none -> 242 us  [the longest x16 123 us: shift_y(): return lax.ppermute(x, 'width', [(i, (i + 2) % n) for i in range(n)])]
    ppermute x0 -> x65, starting transfers between devices: none -> 66 us  [the longest x16 22 us: shift_core(): return lax.ppermute(x, 'width', [(i, i ^ 1) for i in range(n)])]
    dot_general x9 -> x18, matrix products: 147 us -> 175 us  [matmul(): lax.dot_general(left, right, (dims, ((), ())), preferred_element_type=F32)]
    unnamed x7 -> x100, local copies, waits for them, and re-layouts: 31.8 us -> 6.14 us
  transfers between devices with their start and end apart: 5 -> 65, of which waited for: 4 -> 32; matrix products, arithmetic and copies ran while one was open for 5% -> 32% of each run, Pallas kernels for 0% -> 0%
where the time goes in v1:
time: 553 us; the launch traced here: 543 us
  waiting for transfers between devices  242 us (44%)
  matrix products  175 us (32%)
  starting transfers between devices  66 us (12%)
  local copies, waits for them, and re-layouts  29.1 us (5%)
  other arithmetic  28 us (5%)
    dot_general x18, matrix products, matmul(): lax.dot_general(left, right, (dims, ((), ())), preferred_element_type=F32)  175 us
    ppermute x16, waiting for transfers between devices, shift_y(): return lax.ppermute(x, 'width', [(i, (i + 2) % n) for i in range(n)])  123 us
    ppermute x24, waiting for transfers between devices, shift_z(): return lax.ppermute(x, 'hidden', [(i, (i + step) % n) for i in range(n)])  86.1 us
    ppermute x9, waiting for transfers between devices, shift_dp(): return lax.ppermute(x, 'dp', [(i, (i + 1) % n) for i in range(n)])  32.8 us
    ppermute x16, starting transfers between devices, shift_core(): return lax.ppermute(x, 'width', [(i, i ^ 1) for i in range(n)])  22 us
    ppermute x24, starting transfers between devices, shift_z(): return lax.ppermute(x, 'hidden', [(i, (i + step) % n) for i in range(n)])  21.1 us
    ppermute x16, starting transfers between devices, shift_y(): return lax.ppermute(x, 'width', [(i, (i + 2) % n) for i in range(n)])  17.5 us
    squeeze x10, local copies, waits for them, and re-layouts, reduce_width(): x = add(x[:, 0], shift_core(x[:, 1]))  13.2 us
  transfers between devices with their start and end apart: 65, of which 32 were waited for; matrix products, arithmetic and copies ran while one was open for 32% of the time, Pallas kernels for 0%

profile of v1, /device:TPU:1, one launch (start us, length us, event | category | flops | bytes accessed | tf_op | source)
XLA Modules:
  0.0 542.6 jit_solution(16207111001520997999)
XLA Ops:
  5.3 9.9 %convolution_convert_fusion.9 = bf16[256,3584]{1,0:T(8,128)(2,1)S(1)} fusion(bf16[2048,3584]{1,0:T(8,128)(2,1)} %param.8, bf16[512,2048]{1,0:T(8,128)(2,1)S(1)} %convolution_convert_fusion.13), kind=kOutput, calls=%fused_computation.11 | convolution fusion | flops 3759013888 | bytes 17563648 | tf_op jit(solution)/shard_map/dot_general | solution.py:15
  22.9 9.1 %convolution_convert_fusion.7 = bf16[256,3584]{1,0:T(8,128)(2,1)S(1)} fusion(bf16[2048,3584]{1,0:T(8,128)(2,1)} %param.11, bf16[512,2048]{1,0:T(8,128)(2,1)S(1)} %convolution_convert_fusion.13), kind=kOutput, calls=%fused_computation.9 | convolution fusion | flops 3759013888 | bytes 17563648 | tf_op jit(solution)/shard_map/dot_general | solution.py:15
  39.7 10.1 %convolution_convert_fusion.3 = bf16[256,3584]{1,0:T(8,128)(2,1)S(1)} fusion(bf16[2048,3584]{1,0:T(8,128)(2,1)} %param.11, bf16[512,2048]{1,0:T(8,128)(2,1)S(1)} %convolution_convert_fusion.13), kind=kOutput, calls=%fused_computation.5 | convolution fusion | flops 3759013888 | bytes 17563648 | tf_op jit(solution)/shard_map/dot_general | solution.py:15
  77.4 8.6 %collective-permute-done.4 = bf16[64,3584]{1,0:T(8,128)(2,1)S(1)} collective-permute-done((bf16[64,3584]{1,0:T(8,128)(2,1)S(1)}, bf16[64,3584]{1,0:T(8,128)(2,1)S(1)}, u32[]{:S(2)}, u32[]{:S(2)}) %collective-permute-start.4) | collective-permute-done | bytes 458784 | tf_op jit(solution)/shard_map/ppermute | solution.py:25
  87.2 8.5 %collective-permute-done.6 = bf16[64,3584]{1,0:T(8,128)(2,1)S(1)} collective-permute-done((bf16[64,3584]{1,0:T(8,128)(2,1)S(1)}, bf16[64,3584]{1,0:T(8,128)(2,1)S(1)}, u32[]{:S(2)}, u32[]{:S(2)}) %collective-permute-start.6) | collective-permute-done | bytes 458784 | tf_op jit(solution)/shard_map/ppermute | solution.py:25
  97.9 7.6 %collective-permute-done.24 = bf16[64,3584]{1,0:T(8,128)(2,1)S(1)} collective-permute-done((bf16[64,3584]{1,0:T(8,128)(2,1)S(1)}, bf16[64,3584]{1,0:T(8,128)(2,1)S(1)}, u32[]{:S(2)}, u32[]{:S(2)}) %collective-permute-start.24) | collective-permute-done | bytes 458784 | tf_op jit(solution)/shard_map/ppermute | solution.py:25
  105.5 9.8 %collective-permute-done.26 = bf16[64,3584]{1,0:T(8,128)(2,1)S(1)} collective-permute-done((bf16[64,3584]{1,0:T(8,128)(2,1)S(1)}, bf16[64,3584]{1,0:T(8,128)(2,1)S(1)}, u32[]{:S(2)}, u32[]{:S(2)}) %collective-permute-start.26) | collective-permute-done | bytes 458784 | tf_op jit(solution)/shard_map/ppermute | solution.py:25
  115.4 9.8 %collective-permute-done.22 = bf16[64,3584]{1,0:T(8,128)(2,1)S(1)} collective-permute-done((bf16[64,3584]{1,0:T(8,128)(2,1)S(1)}, bf16[64,3584]{1,0:T(8,128)(2,1)S(1)}, u32[]{:S(2)}, u32[]{:S(2)}) %collective-permute-start.22) | collective-permute-done | bytes 458784 | tf_op jit(solution)/shard_map/ppermute | solution.py:25
  128.4 16.5 %collective-permute-done.7 = bf16[2,64,3584]{2,1,0:T(8,128)(2,1)S(1)} collective-permute-done((bf16[2,64,3584]{2,1,0:T(8,128)(2,1)S(1)}, bf16[2,64,3584]{2,1,0:T(8,128)(2,1)S(1)}, u32[]{:S(2)}, u32[]{:S(2)}) %collective-permute-start.7) | collective-permute-done | bytes 917536 | tf_op jit(solution)/shard_map/ppermute | solution.py:25
  149.7 5.9 %convolution_convert_fusion.12 = bf16[512,2048]{1,0:T(8,128)(2,1)} fusion(bf16[512,2048]{1,0:T(8,128)(2,1)S(1)} %copy-done.41, s32[512]{0:T(512)S(1)} %get-tuple-element.42, s32[512]{0:T(512)S(1)} %get-tuple-element.45, s32[]{:T(128)S(6)} %axis_index.35, s32[512]{0:T(512)S(1)} %get-tuple-element.41, s32[512]{0:T(512)S(1)} %get-tuple-element.50, ...), kind=kOutput, calls=%fused_computation.20 | convolution fusion | flops 1096548352 | bytes 4217356 | tf_op jit(solution)/shard_map/dot_general | solution.py:15
  157.4 7.3 %collective-permute-done.27 = bf16[2,64,3584]{2,1,0:T(8,128)(2,1)} collective-permute-done((bf16[2,64,3584]{2,1,0:T(8,128)(2,1)}, bf16[2,64,3584]{2,1,0:T(8,128)(2,1)}, u32[]{:S(2)}, u32[]{:S(2)}) %collective-permute-start.27) | collective-permute-done | bytes 917536 | tf_op jit(solution)/shard_map/ppermute | solution.py:25
  169.6 11.3 %convolution_convert_fusion.11 = bf16[512,2048]{1,0:T(8,128)(2,1)S(1)} fusion(bf16[512,3584]{1,0:T(8,128)(2,1)S(1)} %bitcast.500, bf16[3584,2048]{1,0:T(8,128)(2,1)} %param.10), kind=kOutput, calls=%fused_computation.19 | convolution fusion | flops 7517241344 | bytes 20447232 | tf_op jit(solution)/shard_map/dot_general | solution.py:15
  185.4 11.3 %convolution_convert_fusion.10 = bf16[512,2048]{1,0:T(8,128)(2,1)S(1)} fusion(bf16[512,3584]{1,0:T(8,128)(2,1)S(1)} %bitcast.501, bf16[3584,2048]{1,0:T(8,128)(2,1)} %param.10), kind=kOutput, calls=%fused_computation.18 | convolution fusion | flops 7517241344 | bytes 20447232 | tf_op jit(solution)/shard_map/dot_general | solution.py:15
  206.1 11.1 %collective-permute-done.10 = bf16[4,16,2048]{2,1,0:T(8,128)(2,1)S(1)} collective-permute-done((bf16[4,16,2048]{2,1,0:T(8,128)(2,1)S(1)}, bf16[4,16,2048]{2,1,0:T(8,128)(2,1)S(1)}, u32[]{:S(2)}, u32[]{:S(2)}) %collective-permute-start.10) | collective-permute-done | bytes 262176 | tf_op jit(solution)/shard_map/ppermute | solution.py:30
  237.7 9.6 %collective-permute-done.42 = bf16[4,16,2048]{2,1,0:T(8,128)(2,1)S(1)} collective-permute-done((bf16[4,16,2048]{2,1,0:T(8,128)(2,1)S(1)}, bf16[4,16,2048]{2,1,0:T(8,128)(2,1)S(1)}, u32[]{:S(2)}, u32[]{:S(2)}) %collective-permute-start.42) | collective-permute-done | bytes 262176 | tf_op jit(solution)/shard_map/ppermute | solution.py:30
  247.3 10.2 %collective-permute-done.54 = bf16[4,16,2048]{2,1,0:T(8,128)(2,1)S(1)} collective-permute-done((bf16[4,16,2048]{2,1,0:T(8,128)(2,1)S(1)}, bf16[4,16,2048]{2,1,0:T(8,128)(2,1)S(1)}, u32[]{:S(2)}, u32[]{:S(2)}) %collective-permute-start.54) | collective-permute-done | bytes 262176 | tf_op jit(solution)/shard_map/ppermute | solution.py:30
  263.3 10.3 %collective-permute-done.13 = bf16[4,16,2048]{2,1,0:T(8,128)(2,1)S(1)} collective-permute-done((bf16[4,16,2048]{2,1,0:T(8,128)(2,1)S(1)}, bf16[4,16,2048]{2,1,0:T(8,128)(2,1)S(1)}, u32[]{:S(2)}, u32[]{:S(2)}) %collective-permute-start.13) | collective-permute-done | bytes 262176 | tf_op jit(solution)/shard_map/ppermute | solution.py:30
  279.3 11.2 %collective-permute-done.14 = bf16[4,16,2048]{2,1,0:T(8,128)(2,1)S(1)} collective-permute-done((bf16[4,16,2048]{2,1,0:T(8,128)(2,1)S(1)}, bf16[4,16,2048]{2,1,0:T(8,128)(2,1)S(1)}, u32[]{:S(2)}, u32[]{:S(2)}) %collective-permute-start.14) | collective-permute-done | bytes 262176 | tf_op jit(solution)/shard_map/ppermute | solution.py:30
  290.6 16.2 %convolution_convert_fusion.6 = bf16[256,3584]{1,0:T(8,128)(2,1)} fusion(bf16[256,2048]{1,0:T(8,128)(2,1)S(1)} %bitcast.546, bf16[3584,2048]{1,0:T(8,128)(2,1)} %param.10), kind=kOutput, calls=%fused_computation.8 | convolution fusion | flops 3759013888 | bytes 17563648 | tf_op jit(solution)/shard_map/dot_general | solution.py:15
  312.8 16.2 %convolution_convert_fusion.2 = bf16[256,3584]{1,0:T(8,128)(2,1)} fusion(bf16[256,2048]{1,0:T(8,128)(2,1)S(1)} %bitcast.545, bf16[3584,2048]{1,0:T(8,128)(2,1)} %param.10), kind=kOutput, calls=%fused_computation.4 | convolution fusion | flops 3759013888 | bytes 17563648 | tf_op jit(solution)/shard_map/dot_general | solution.py:15
  343.5 16.2 %convolution_convert_fusion.1 = bf16[256,3584]{1,0:T(8,128)(2,1)} fusion(bf16[256,2048]{1,0:T(8,128)(2,1)S(1)} %bitcast.547, bf16[3584,2048]{1,0:T(8,128)(2,1)} %param.10), kind=kOutput, calls=%fused_computation.3 | convolution fusion | flops 3759013888 | bytes 17563648 | tf_op jit(solution)/shard_map/dot_general | solution.py:15
  363.3 16.3 %convolution_convert_fusion = bf16[256,3584]{1,0:T(8,128)(2,1)} fusion(bf16[256,2048]{1,0:T(8,128)(2,1)S(1)} %bitcast.548, bf16[3584,2048]{1,0:T(8,128)(2,1)} %param.10), kind=kOutput, calls=%fused_computation.2 | convolution fusion | flops 3759013888 | bytes 17563648 | tf_op jit(solution)/shard_map/dot_general | solution.py:15
  395.2 19.7 %collective-permute-done.48 = bf16[64,3584]{1,0:T(8,128)(2,1)S(1)} collective-permute-done((bf16[64,3584]{1,0:T(8,128)(2,1)S(1)}, bf16[64,3584]{1,0:T(8,128)(2,1)S(1)}, u32[]{:S(2)}, u32[]{:S(2)}) %collective-permute-start.48) | collective-permute-done | bytes 458784 | tf_op jit(solution)/shard_map/ppermute | solution.py:25
  417.6 7.1 %collective-permute-done.60 = bf16[64,3584]{1,0:T(8,128)(2,1)S(1)} collective-permute-done((bf16[64,3584]{1,0:T(8,128)(2,1)S(1)}, bf16[64,3584]{1,0:T(8,128)(2,1)S(1)}, u32[]{:S(2)}, u32[]{:S(2)}) %collective-permute-start.60) | collective-permute-done | bytes 458784 | tf_op jit(solution)/shard_map/ppermute | solution.py:25
  427.6 6.9 %collective-permute-done.49 = bf16[64,3584]{1,0:T(8,128)(2,1)S(1)} collective-permute-done((bf16[64,3584]{1,0:T(8,128)(2,1)S(1)}, bf16[64,3584]{1,0:T(8,128)(2,1)S(1)}, u32[]{:S(2)}, u32[]{:S(2)}) %collective-permute-start.49) | collective-permute-done | bytes 458784 | tf_op jit(solution)/shard_map/ppermute | solution.py:25
  436.4 8.0 %collective-permute-done.61 = bf16[64,3584]{1,0:T(8,128)(2,1)S(1)} collective-permute-done((bf16[64,3584]{1,0:T(8,128)(2,1)S(1)}, bf16[64,3584]{1,0:T(8,128)(2,1)S(1)}, u32[]{:S(2)}, u32[]{:S(2)}) %collective-permute-start.61) | collective-permute-done | bytes 458784 | tf_op jit(solution)/shard_map/ppermute | solution.py:25
  454.5 12.5 %collective-permute-done.63 = bf16[64,3584]{1,0:T(8,128)(2,1)S(1)} collective-permute-done((bf16[64,3584]{1,0:T(8,128)(2,1)S(1)}, bf16[64,3584]{1,0:T(8,128)(2,1)S(1)}, u32[]{:S(2)}, u32[]{:S(2)}) %collective-permute-start.63) | collective-permute-done | bytes 458784 | tf_op jit(solution)/shard_map/ppermute | solution.py:35
  477.6 9.1 %collective-permute-done.38 = bf16[64,3584]{1,0:T(8,128)(2,1)S(1)} collective-permute-done((bf16[64,3584]{1,0:T(8,128)(2,1)S(1)}, bf16[64,3584]{1,0:T(8,128)(2,1)S(1)}, u32[]{:S(2)}, u32[]{:S(2)}) %collective-permute-start.38) | collective-permute-done | bytes 458784 | tf_op jit(solution)/shard_map/ppermute | solution.py:35
  504.9 7.4 %fusion.53 = f32[1024,3584]{1,0:T(8,128)} fusion(bf16[512,3584]{1,0:T(8,128)(2,1)S(1)} %bitcast.498, bf16[256,1024]{1,0:T(8,128)(2,1)S(1)} %get-tuple-element.35, bf16[256,1024]{1,0:T(8,128)(2,1)S(1)} %get-tuple-element.11), kind=kOutput, calls=%fused_computation.179 | convolution fusion | flops 3760193536 | bytes 19398656 | tf_op jit(solution)/shard_map/dot_general | solution.py:15
  512.3 7.5 %fusion.54 = f32[1024,3584]{1,0:T(8,128)} fusion(bf16[512,3584]{1,0:T(8,128)(2,1)S(1)} %bitcast.499, bf16[256,1024]{1,0:T(8,128)(2,1)S(1)} %get-tuple-element.35, bf16[256,1024]{1,0:T(8,128)(2,1)S(1)} %get-tuple-element.11), kind=kOutput, calls=%fused_computation.180 | convolution fusion | flops 3760193536 | bytes 19398656 | tf_op jit(solution)/shard_map/dot_general | solution.py:15
  519.8 12.0 %multiply_convert_fusion = bf16[1024,3584]{1,0:T(8,128)(2,1)} fusion(f32[1024,3584]{1,0:T(8,128)} %fusion.53, bf16[512,3584]{1,0:T(8,128)(2,1)S(1)} %bitcast.496, bf16[2048,3584]{1,0:T(8,128)(2,1)} %param.11, s32[]{:T(128)S(6)} %select_n.75, bf16[256,1024]{1,0:T(8,128)(2,1)S(1)} %get-tuple-element.34, bf16[256,1024]{1,0:T(8,128)(2,1)S(1)} %get-tuple-element.10), kind=kOutput, calls=%fused_computation | convolution fusion | flops 3782213632 | bytes 34078724 | tf_op jit(solution)/shard_map/dot_general | solution.py:15
  531.8 10.4 %multiply_convert_fusion.1 = bf16[1024,3584]{1,0:T(8,128)(2,1)} fusion(f32[1024,3584]{1,0:T(8,128)} %fusion.54, bf16[512,3584]{1,0:T(8,128)(2,1)} %bitcast.497, bf16[256,1024]{1,0:T(8,128)(2,1)S(1)} %get-tuple-element.34, bf16[256,1024]{1,0:T(8,128)(2,1)S(1)} %get-tuple-element.10), kind=kOutput, calls=%fused_computation.1 | convolution fusion | flops 3771203584 | bytes 26738688 | tf_op jit(solution)/shard_map/dot_general | solution.py:15
  (301 shorter events, 196.8 us)
Async XLA Ops:
  16.8 41.8 %collective-permute-start.1 = (bf16[2,64,3584]{2,1,0:T(8,128)(2,1)}, bf16[2,64,3584]{2,1,0:T(8,128)(2,1)}, u32[]{:S(2)}, u32[]{:S(2)}) collective-permute-start(bf16[2,64,3584]{2,1,0:T(8,128)(2,1)} %slice_bitcast_fusion.28), channel_id=1, source_target_pairs={{0,4},{4,0},{8,12},{12,8},{1,5},{5,1},{9,13},{13,9},{2,6},{6,2},{1... | collective-permute-start | bytes 2752520 | tf_op jit(solution)/shard_map/ppermute | solution.py:20
  22.4 38.3 %collective-permute-start.3 = (bf16[2,64,3584]{2,1,0:T(8,128)(2,1)}, bf16[2,64,3584]{2,1,0:T(8,128)(2,1)}, u32[]{:S(2)}, u32[]{:S(2)}) collective-permute-start(bf16[2,64,3584]{2,1,0:T(8,128)(2,1)} %slice_bitcast_fusion.25), channel_id=1, source_target_pairs={{0,4},{4,0},{8,12},{12,8},{1,5},{5,1},{9,13},{13,9},{2,6},{6,2},{1... | collective-permute-start | bytes 2752520 | tf_op jit(solution)/shard_map/ppermute | solution.py:20
  33.6 30.9 %collective-permute-start.5 = (bf16[2,64,3584]{2,1,0:T(8,128)(2,1)}, bf16[2,64,3584]{2,1,0:T(8,128)(2,1)S(1)}, u32[]{:S(2)}, u32[]{:S(2)}) collective-permute-start(bf16[2,64,3584]{2,1,0:T(8,128)(2,1)} %slice_bitcast_fusion.22), channel_id=1, source_target_pairs={{0,4},{4,0},{8,12},{12,8},{1,5},{5,1},{9,13},{13,9},{2,6},{6,2},{1... | collective-permute-start | bytes 2752520 | tf_op jit(solution)/shard_map/ppermute | solution.py:20
  39.2 27.0 %collective-permute-start.23 = (bf16[2,64,3584]{2,1,0:T(8,128)(2,1)}, bf16[2,64,3584]{2,1,0:T(8,128)(2,1)}, u32[]{:S(2)}, u32[]{:S(2)}) collective-permute-start(bf16[2,64,3584]{2,1,0:T(8,128)(2,1)} %slice_bitcast_fusion.13), channel_id=1, source_target_pairs={{0,4},{4,0},{8,12},{12,8},{1,5},{5,1},{9,13},{13,9},{2,6},{6,2},{1... | collective-permute-start | bytes 2752520 | tf_op jit(solution)/shard_map/ppermute | solution.py:20
  60.7 438.6 %collective-permute-start = (bf16[512,1024]{1,0:T(8,128)(2,1)}, bf16[512,1024]{1,0:T(8,128)(2,1)}, u32[]{:S(2)}, u32[]{:S(2)}) collective-permute-start(bf16[512,1024]{1,0:T(8,128)(2,1)} %constant_dynamic-slice_fusion.1), channel_id=1, source_target_pairs={{0,16},{16,0},{1,17},{17,1},{2,18},{18,2},{3,19},{19,3},{4,20},{20... | collective-permute-start | bytes 3145736 | tf_op jit(solution)/shard_map/ppermute | solution.py:35
  68.9 26.8 %collective-permute-start.6 = (bf16[64,3584]{1,0:T(8,128)(2,1)S(1)}, bf16[64,3584]{1,0:T(8,128)(2,1)S(1)}, u32[]{:S(2)}, u32[]{:S(2)}) collective-permute-start(bf16[64,3584]{1,0:T(8,128)(2,1)S(1)} %fusion.71), channel_id=1, source_target_pairs={{0,8},{4,12},{8,0},{12,4},{1,9},{5,13},{9,1},{13,5},{2,10},{6,14},... | collective-permute-start | bytes 1376264 | tf_op jit(solution)/shard_map/ppermute | solution.py:25
  71.7 33.9 %collective-permute-start.24 = (bf16[64,3584]{1,0:T(8,128)(2,1)S(1)}, bf16[64,3584]{1,0:T(8,128)(2,1)S(1)}, u32[]{:S(2)}, u32[]{:S(2)}) collective-permute-start(bf16[64,3584]{1,0:T(8,128)(2,1)S(1)} %fusion.74), channel_id=1, source_target_pairs={{0,8},{4,12},{8,0},{12,4},{1,9},{5,13},{9,1},{13,5},{2,10},{6,14},... | collective-permute-start | bytes 1376264 | tf_op jit(solution)/shard_map/ppermute | solution.py:25
  76.2 39.2 %collective-permute-start.26 = (bf16[64,3584]{1,0:T(8,128)(2,1)S(1)}, bf16[64,3584]{1,0:T(8,128)(2,1)S(1)}, u32[]{:S(2)}, u32[]{:S(2)}) collective-permute-start(bf16[64,3584]{1,0:T(8,128)(2,1)S(1)} %fusion.75), channel_id=1, source_target_pairs={{0,8},{4,12},{8,0},{12,4},{1,9},{5,13},{9,1},{13,5},{2,10},{6,14},... | collective-permute-start | bytes 1376264 | tf_op jit(solution)/shard_map/ppermute | solution.py:25
  86.0 39.2 %collective-permute-start.22 = (bf16[64,3584]{1,0:T(8,128)(2,1)S(1)}, bf16[64,3584]{1,0:T(8,128)(2,1)S(1)}, u32[]{:S(2)}, u32[]{:S(2)}) collective-permute-start(bf16[64,3584]{1,0:T(8,128)(2,1)S(1)} %fusion.73), channel_id=1, source_target_pairs={{0,8},{4,12},{8,0},{12,4},{1,9},{5,13},{9,1},{13,5},{2,10},{6,14},... | collective-permute-start | bytes 1376264 | tf_op jit(solution)/shard_map/ppermute | solution.py:25
  96.6 48.2 %collective-permute-start.7 = (bf16[2,64,3584]{2,1,0:T(8,128)(2,1)S(1)}, bf16[2,64,3584]{2,1,0:T(8,128)(2,1)S(1)}, u32[]{:S(2)}, u32[]{:S(2)}) collective-permute-start(bf16[2,64,3584]{2,1,0:T(8,128)(2,1)S(1)} %get-tuple-element.37), channel_id=1, source_target_pairs={{0,8},{4,12},{8,0},{12,4},{1,9},{5,13},{9,1},{13,5},{2,10},{6,14},... | collective-permute-start | bytes 2752520 | tf_op jit(solution)/shard_map/ppermute | solution.py:25
  127.1 37.5 %collective-permute-start.27 = (bf16[2,64,3584]{2,1,0:T(8,128)(2,1)}, bf16[2,64,3584]{2,1,0:T(8,128)(2,1)}, u32[]{:S(2)}, u32[]{:S(2)}) collective-permute-start(bf16[2,64,3584]{2,1,0:T(8,128)(2,1)} %get-tuple-element.39), channel_id=1, source_target_pairs={{0,8},{4,12},{8,0},{12,4},{1,9},{5,13},{9,1},{13,5},{2,10},{6,14},... | collective-permute-start | bytes 2752520 | tf_op jit(solution)/shard_map/ppermute | solution.py:25
  182.3 40.7 %collective-permute-start.41 = (bf16[4,16,2048]{2,1,0:T(8,128)(2,1)S(1)}, bf16[4,16,2048]{2,1,0:T(8,128)(2,1)S(1)}, u32[]{:S(2)}, u32[]{:S(2)}) collective-permute-start(bf16[4,16,2048]{2,1,0:T(8,128)(2,1)S(1)} %get-tuple-element.17), channel_id=1, source_target_pairs={{0,3},{1,0},{2,1},{3,2},{4,7},{5,4},{6,5},{7,6},{8,11},{9,8},{10,9... | collective-permute-start | bytes 786440 | tf_op jit(solution)/shard_map/ppermute | solution.py:30
  196.8 35.1 %collective-permute-start.53 = (bf16[4,16,2048]{2,1,0:T(8,128)(2,1)S(1)}, bf16[4,16,2048]{2,1,0:T(8,128)(2,1)S(1)}, u32[]{:S(2)}, u32[]{:S(2)}) collective-permute-start(bf16[4,16,2048]{2,1,0:T(8,128)(2,1)S(1)} %get-tuple-element.21), channel_id=1, source_target_pairs={{0,3},{1,0},{2,1},{3,2},{4,7},{5,4},{6,5},{7,6},{8,11},{9,8},{10,9... | collective-permute-start | bytes 786440 | tf_op jit(solution)/shard_map/ppermute | solution.py:30
  228.6 29.0 %collective-permute-start.12 = (bf16[4,16,2048]{2,1,0:T(8,128)(2,1)S(1)}, bf16[4,16,2048]{2,1,0:T(8,128)(2,1)S(1)}, u32[]{:S(2)}, u32[]{:S(2)}) collective-permute-start(bf16[4,16,2048]{2,1,0:T(8,128)(2,1)S(1)} %get-tuple-element.12), channel_id=1, source_target_pairs={{0,1},{1,2},{2,3},{3,0},{4,5},{5,6},{6,7},{7,4},{8,9},{9,10},{10,1... | collective-permute-start | bytes 786440 | tf_op jit(solution)/shard_map/ppermute | solution.py:30
  234.3 24.8 %collective-permute-start.32 = (bf16[4,16,2048]{2,1,0:T(8,128)(2,1)S(1)}, bf16[4,16,2048]{2,1,0:T(8,128)(2,1)S(1)}, u32[]{:S(2)}, u32[]{:S(2)}) collective-permute-start(bf16[4,16,2048]{2,1,0:T(8,128)(2,1)S(1)} %get-tuple-element.18), channel_id=1, source_target_pairs={{0,1},{1,2},{2,3},{3,0},{4,5},{5,6},{6,7},{7,4},{8,9},{9,10},{10,1... | collective-permute-start | bytes 786440 | tf_op jit(solution)/shard_map/ppermute | solution.py:30
  234.4 23.1 %collective-permute-start.54 = (bf16[4,16,2048]{2,1,0:T(8,128)(2,1)S(1)}, bf16[4,16,2048]{2,1,0:T(8,128)(2,1)S(1)}, u32[]{:S(2)}, u32[]{:S(2)}) collective-permute-start(bf16[4,16,2048]{2,1,0:T(8,128)(2,1)S(1)} %get-tuple-element.19), channel_id=1, source_target_pairs={{0,3},{1,0},{2,1},{3,2},{4,7},{5,4},{6,5},{7,6},{8,11},{9,8},{10,9... | collective-permute-start | bytes 786440 | tf_op jit(solution)/shard_map/ppermute | solution.py:30
  263.2 49.3 %collective-permute-start.44 = (bf16[4,16,2048]{2,1,0:T(8,128)(2,1)S(1)}, bf16[4,16,2048]{2,1,0:T(8,128)(2,1)}, u32[]{:S(2)}, u32[]{:S(2)}) collective-permute-start(bf16[4,16,2048]{2,1,0:T(8,128)(2,1)S(1)} %fusion.60), channel_id=1, source_target_pairs={{0,3},{1,0},{2,1},{3,2},{4,7},{5,4},{6,5},{7,6},{8,11},{9,8},{10,9... | collective-permute-start | bytes 786440 | tf_op jit(solution)/shard_map/ppermute | solution.py:30
  273.7 55.3 %collective-permute-start.56 = (bf16[4,16,2048]{2,1,0:T(8,128)(2,1)S(1)}, bf16[4,16,2048]{2,1,0:T(8,128)(2,1)S(1)}, u32[]{:S(2)}, u32[]{:S(2)}) collective-permute-start(bf16[4,16,2048]{2,1,0:T(8,128)(2,1)S(1)} %fusion.57), channel_id=1, source_target_pairs={{0,3},{1,0},{2,1},{3,2},{4,7},{5,4},{6,5},{7,6},{8,11},{9,8},{10,9... | collective-permute-start | bytes 786440 | tf_op jit(solution)/shard_map/ppermute | solution.py:30
  279.3 32.1 %collective-permute-start.34 = (bf16[4,16,2048]{2,1,0:T(8,128)(2,1)}, bf16[4,16,2048]{2,1,0:T(8,128)(2,1)}, u32[]{:S(2)}, u32[]{:S(2)}) collective-permute-start(bf16[4,16,2048]{2,1,0:T(8,128)(2,1)} %collective-permute-done.33), channel_id=1, source_target_pairs={{0,1},{1,2},{2,3},{3,0},{4,5},{5,6},{6,7},{7,4},{8,9},{9,10},{10,1... | collective-permute-start | bytes 786440 | tf_op jit(solution)/shard_map/ppermute | solution.py:30
  309.0 72.1 %collective-permute-start.15 = (bf16[2,64,3584]{2,1,0:T(8,128)(2,1)}, bf16[2,64,3584]{2,1,0:T(8,128)(2,1)}, u32[]{:S(2)}, u32[]{:S(2)}) collective-permute-start(bf16[2,64,3584]{2,1,0:T(8,128)(2,1)} %slice_bitcast_fusion.19), channel_id=1, source_target_pairs={{0,4},{4,0},{8,12},{12,8},{1,5},{5,1},{9,13},{13,9},{2,6},{6,2},{1... | collective-permute-start | bytes 2752520 | tf_op jit(solution)/shard_map/ppermute | solution.py:20
  331.4 52.9 %collective-permute-start.35 = (bf16[2,64,3584]{2,1,0:T(8,128)(2,1)}, bf16[2,64,3584]{2,1,0:T(8,128)(2,1)}, u32[]{:S(2)}, u32[]{:S(2)}) collective-permute-start(bf16[2,64,3584]{2,1,0:T(8,128)(2,1)} %slice_bitcast_fusion.7), channel_id=1, source_target_pairs={{0,4},{4,0},{8,12},{12,8},{1,5},{5,1},{9,13},{13,9},{2,6},{6,2},{1... | collective-permute-start | bytes 2752520 | tf_op jit(solution)/shard_map/ppermute | solution.py:20
  336.8 26.3 %collective-permute-start.58 = (bf16[4,16,2048]{2,1,0:T(8,128)(2,1)S(1)}, bf16[4,16,2048]{2,1,0:T(8,128)(2,1)S(1)}, u32[]{:S(2)}, u32[]{:S(2)}) collective-permute-start(bf16[4,16,2048]{2,1,0:T(8,128)(2,1)S(1)} %collective-permute-done.57), channel_id=1, source_target_pairs={{0,3},{1,0},{2,1},{3,2},{4,7},{5,4},{6,5},{7,6},{8,11},{9,8},{10,9... | collective-permute-start | bytes 786440 | tf_op jit(solution)/shard_map/ppermute | solution.py:30
  361.9 24.4 %collective-permute-start.47 = (bf16[2,64,3584]{2,1,0:T(8,128)(2,1)}, bf16[2,64,3584]{2,1,0:T(8,128)(2,1)}, u32[]{:S(2)}, u32[]{:S(2)}) collective-permute-start(bf16[2,64,3584]{2,1,0:T(8,128)(2,1)} %slice_bitcast_fusion.4), channel_id=1, source_target_pairs={{0,4},{4,0},{8,12},{12,8},{1,5},{5,1},{9,13},{13,9},{2,6},{6,2},{1... | collective-permute-start | bytes 2752520 | tf_op jit(solution)/shard_map/ppermute | solution.py:20
  385.8 31.8 %collective-permute-start.36 = (bf16[64,3584]{1,0:T(8,128)(2,1)S(1)}, bf16[64,3584]{1,0:T(8,128)(2,1)S(1)}, u32[]{:S(2)}, u32[]{:S(2)}) collective-permute-start(bf16[64,3584]{1,0:T(8,128)(2,1)S(1)} %fusion.76), channel_id=1, source_target_pairs={{0,8},{4,12},{8,0},{12,4},{1,9},{5,13},{9,1},{13,5},{2,10},{6,14},... | collective-permute-start | bytes 1376264 | tf_op jit(solution)/shard_map/ppermute | solution.py:25
  387.9 27.0 %collective-permute-start.48 = (bf16[64,3584]{1,0:T(8,128)(2,1)S(1)}, bf16[64,3584]{1,0:T(8,128)(2,1)S(1)}, u32[]{:S(2)}, u32[]{:S(2)}) collective-permute-start(bf16[64,3584]{1,0:T(8,128)(2,1)S(1)} %fusion.77), channel_id=1, source_target_pairs={{0,8},{4,12},{8,0},{12,4},{1,9},{5,13},{9,1},{13,5},{2,10},{6,14},... | collective-permute-start | bytes 1376264 | tf_op jit(solution)/shard_map/ppermute | solution.py:25
  389.3 35.4 %collective-permute-start.60 = (bf16[64,3584]{1,0:T(8,128)(2,1)S(1)}, bf16[64,3584]{1,0:T(8,128)(2,1)S(1)}, u32[]{:S(2)}, u32[]{:S(2)}) collective-permute-start(bf16[64,3584]{1,0:T(8,128)(2,1)S(1)} %fusion.78), channel_id=1, source_target_pairs={{0,8},{4,12},{8,0},{12,4},{1,9},{5,13},{9,1},{13,5},{2,10},{6,14},... | collective-permute-start | bytes 1376264 | tf_op jit(solution)/shard_map/ppermute | solution.py:25
  427.1 21.0 %collective-permute-start.62 = (bf16[64,3584]{1,0:T(8,128)(2,1)S(1)}, bf16[64,3584]{1,0:T(8,128)(2,1)S(1)}, u32[]{:S(2)}, u32[]{:S(2)}) collective-permute-start(bf16[64,3584]{1,0:T(8,128)(2,1)S(1)} %get-tuple-element.4), channel_id=1, source_target_pairs={{0,16},{16,0},{1,17},{17,1},{2,18},{18,2},{3,19},{19,3},{4,20},{20... | collective-permute-start | bytes 1376264 | tf_op jit(solution)/shard_map/ppermute | solution.py:35
  444.4 27.5 %collective-permute-start.18 = (bf16[64,3584]{1,0:T(8,128)(2,1)S(1)}, bf16[64,3584]{1,0:T(8,128)(2,1)S(1)}, u32[]{:S(2)}, u32[]{:S(2)}) collective-permute-start(bf16[64,3584]{1,0:T(8,128)(2,1)S(1)} %fusion.17), channel_id=1, source_target_pairs={{0,16},{16,0},{1,17},{17,1},{2,18},{18,2},{3,19},{19,3},{4,20},{20... | collective-permute-start | bytes 1376264 | tf_op jit(solution)/shard_map/ppermute | solution.py:35
  448.1 25.1 %collective-permute-start.37 = (bf16[64,3584]{1,0:T(8,128)(2,1)S(1)}, bf16[64,3584]{1,0:T(8,128)(2,1)S(1)}, u32[]{:S(2)}, u32[]{:S(2)}) collective-permute-start(bf16[64,3584]{1,0:T(8,128)(2,1)S(1)} %fusion.20), channel_id=1, source_target_pairs={{0,8},{4,12},{8,0},{12,4},{1,9},{5,13},{9,1},{13,5},{2,10},{6,14},... | collective-permute-start | bytes 1376264 | tf_op jit(solution)/shard_map/ppermute | solution.py:25
  454.2 22.7 %collective-permute-start.19 = (bf16[64,3584]{1,0:T(8,128)(2,1)S(1)}, bf16[64,3584]{1,0:T(8,128)(2,1)S(1)}, u32[]{:S(2)}, u32[]{:S(2)}) collective-permute-start(bf16[64,3584]{1,0:T(8,128)(2,1)S(1)} %collective-permute-done.17), channel_id=1, source_target_pairs={{0,16},{16,0},{1,17},{17,1},{2,18},{18,2},{3,19},{19,3},{4,20},{20... | collective-permute-start | bytes 1376264 | tf_op jit(solution)/shard_map/ppermute | solution.py:35
  467.0 33.6 %collective-permute-start.52 = (bf16[4,64,3584]{2,1,0:T(8,128)(2,1)S(1)}, bf16[4,64,3584]{2,1,0:T(8,128)(2,1)S(1)}, u32[]{:S(2)}, u32[]{:S(2)}) collective-permute-start(bf16[4,64,3584]{2,1,0:T(8,128)(2,1)S(1)} %get-tuple-element.23), channel_id=1, source_target_pairs={{0,4},{4,0},{8,12},{12,8},{1,5},{5,1},{9,13},{13,9},{2,6},{6,2},{1... | collective-permute-start | bytes 5505032 | tf_op jit(solution)/shard_map/ppermute | solution.py:20
  471.9 29.5 %collective-permute-start.64 = (bf16[4,64,3584]{2,1,0:T(8,128)(2,1)S(1)}, bf16[4,64,3584]{2,1,0:T(8,128)(2,1)S(1)}, u32[]{:S(2)}, u32[]{:S(2)}) collective-permute-start(bf16[4,64,3584]{2,1,0:T(8,128)(2,1)S(1)} %get-tuple-element.25), channel_id=1, source_target_pairs={{0,4},{4,0},{8,12},{12,8},{1,5},{5,1},{9,13},{13,9},{2,6},{6,2},{1... | collective-permute-start | bytes 5505032 | tf_op jit(solution)/shard_map/ppermute | solution.py:20
  (83 other events, 1312.4 us)

commit v2 on v1

--- a/solution.py
+++ b/solution.py
@@ -3,6 +3,8 @@
 import jax
 import jax.numpy as jnp
 from jax import lax
+from jax.experimental import pallas as pl
+from jax.experimental.pallas import tpu as pltpu
 from jax.sharding import PartitionSpec as P
 
 D = 8192
@@ -15,6 +17,37 @@
     return lax.dot_general(left, right, (dims, ((), ())), preferred_element_type=F32).astype(out)
 
 
+def after(x, *others):
+    return lax.optimization_barrier((x, others))[0]
+
+
+def back_kernel(left_ref, right_ref, out_ref):
+    out_ref[...] = lax.dot_general(
+        left_ref[...], right_ref[...], (((1,), (1,)), ((), ())), preferred_element_type=F32
+    ).astype(out_ref.dtype)
+
+
+def matmul_back(left, right):
+    (m, depth), n = left.shape, right.shape[0]
+    tile = 512 if n % 512 == 0 else 256
+    return pl.pallas_call(
+        back_kernel,
+        grid=(n // tile,),
+        in_specs=[
+            pl.BlockSpec((m, depth), lambda i: (0, 0)),
+            pl.BlockSpec((tile, depth), lambda i: (i, 0)),
+        ],
+        out_specs=pl.BlockSpec((m, tile), lambda i: (0, i)),
+        out_shape=jax.ShapeDtypeStruct((m, n), BF16),
+        compiler_params=pltpu.CompilerParams(vmem_limit_bytes=24 * 1024 * 1024),
+        cost_estimate=pl.CostEstimate(
+            flops=2 * m * n * depth,
+            bytes_accessed=2 * (m * depth + n * depth + m * n),
+            transcendentals=0,
+        ),
+    )(left, right)
+
+
 def shift_core(x):
     n = lax.axis_size("width")
     return lax.ppermute(x, "width", [(i, i ^ 1) for i in range(n)])
@@ -39,9 +72,12 @@
     return left.astype(F32) + right.astype(F32)
 
 
-def reduce_width(x):
+def reduce_core(x):
+    return add(x[:, 0], shift_core(x[:, 1]))
+
+
+def reduce_y(x):
     ny = x.shape[0]
-    x = add(x[:, 0], shift_core(x[:, 1]))
     total = x[ny - 1]
     for step in range(ny - 1):
         total = add(x[ny - 2 - step], shift_y(total.astype(BF16)))
@@ -128,52 +164,72 @@
     mine = lax.dynamic_slice_in_dim(tokens, dp * half, half, 1)
     other = shift_dp(lax.dynamic_slice_in_dim(tokens, (1 - dp) * half, half, 1))
 
-    def stage_a(k):
-        tok = tokens[k * t:(k + 1) * t]
-        pre = [
-            reduce_width(matmul(tok, weight).reshape(ny, 2, nz * r, ff))
-            for weight in (gate_weight, up_weight, probe_sign)
-        ]
+    def stage_a(tok):
+        chip = []
+        for weight in (gate_weight, up_weight, probe_sign):
+            held = after(tok, chip[0]) if len(chip) == 2 else tok
+            chip.append(reduce_core(matmul(held, weight).reshape(ny, 2, nz * r, ff)))
+        pre = [reduce_y(part) for part in chip]
         hidden, hidden_dot, c1, c2 = coefficients(pre[0], pre[1], pre[2] * inv_width)
         both = jnp.stack([hidden, hidden_dot])
         own = jnp.stack(gather_width(both, ny), axis=1)
         full = jnp.stack([own, shift_core(own)], axis=2)
-        return full.reshape(2 * t, ff), c1, c2
-
-    def stage_b(k, full):
-        out = matmul(full, down_weight).reshape(2, n_width, nz, r, cols)
-        result = []
+        return full.reshape(2 * t, ff), c1, c2, pre[2]
+
+    def stage_b(k, out):
+        out = out.reshape(2, n_width, nz, r, cols)
+        result, totals = [], []
         for i, step in ((0, 1), (1, -1)):
             total = reduce_hidden([out[i, :, s] for s in range(nz)], step)
             if i == 0:
                 goal = target[k * t:(k + 1) * t].reshape(n_width, nz, r, cols)[:, 0]
                 total = total - goal.astype(F32)
-            pieces = gather_hidden(total.astype(BF16), step, nz)
+            total = total.astype(BF16)
+            totals.append(total)
+            pieces = gather_hidden(total, step, nz)
             result.append(jnp.stack(pieces, axis=1).reshape(t, cols))
-        return result
-
-    def stage_c(resid, output_dot, c1, c2):
-        back, back_dot = [
-            reduce_width(matmul(v, down_weight, ((1,), (1,))).reshape(ny, 2, nz * r, ff))
-            for v in (resid, output_dot)
-        ]
-        result = []
-        for err in errors(back, back_dot, c1, c2):
-            own = gather_width(err, ny)
+        return jnp.concatenate(result), totals
+
+    def stage_c(resid, c1, c2):
+        back = matmul_back(resid, down_weight).reshape(2, ny, 2, nz * r, ff)
+        return errors(reduce_y(reduce_core(back[0])), reduce_y(reduce_core(back[1])), c1, c2)
+
+    def gather_error(err, y_last):
+        own = gather_width(err, ny)
+        if y_last:
+            far = gather_width(shift_dp(err), ny)
+        else:
             far = [shift_dp(piece) for piece in own]
-            part = jnp.stack(own + far)
-            result.append(jnp.stack([part, shift_core(part)], axis=1).reshape(n_dp * t, ff))
-        return result
-
-    a = [stage_a(k) for k in range(CHUNKS)]
-    b = [stage_b(k, a[k][0]) for k in range(CHUNKS)]
-    c = [stage_c(*b[k], a[k][1], a[k][2]) for k in range(CHUNKS)]
-    sums = [None, None]
+        part = jnp.stack(own + far)
+        return jnp.stack([part, shift_core(part)], axis=1).reshape(n_dp * t, ff)
+
+    coeffs, fulls, resids, gathered = [], [], [], []
+    totals = mark = err = None
     for k in range(CHUNKS):
-        tok = jnp.concatenate([mine[k * t:(k + 1) * t], other[k * t:(k + 1) * t]])
-        for i in range(2):
-            term = matmul(tok, c[k][i], ((0,), (0,)), F32)
-            sums[i] = term if sums[i] is None else sums[i] + term
+        tok = tokens[k * t:(k + 1) * t]
+        if k:
+            tok = after(tok, mark)
+        full, c1, c2, mark = stage_a(tok)
+        fulls.append(full)
+        coeffs.append((c1, c2))
+    for k in range(CHUNKS):
+        full = after(fulls[k], *totals) if k else fulls[k]
+        out = matmul(full, down_weight)
+        if k:
+            out = after(out, resids[-1])
+        resid, totals = stage_b(k, out)
+        resids.append(resid)
+    for k in range(CHUNKS):
+        resid = after(resids[k], *err) if k else resids[k]
+        err = stage_c(resid, *coeffs[k])
+        gathered.append([gather_error(err[i], k == CHUNKS - 1 and i == 1) for i in range(2)])
+    tok = jnp.concatenate(
+        [part[k * t:(k + 1) * t] for k in range(CHUNKS) for part in (mine, other)]
+    )
+    sums = [
+        matmul(tok, jnp.concatenate([g[i] for g in gathered]), ((0,), (0,)), F32)
+        for i in range(2)
+    ]
     probe_rows = lax.dynamic_slice_in_dim(probe_sign, dp * half, half, 0)
     gate_grad = (sums[0] * token_scale).astype(BF16)
     hess_diag = (probe_rows.astype(F32) * (sums[1] * token_scale) * inv_width).astype(BF16)

time: 553 us -> 452 us (0.82)
  matrix products: 175 us -> 93 us
  waiting for transfers between devices: 242 us -> 187 us
  starting transfers between devices: 66 us -> 98.4 us
  Pallas kernels: 0 us -> 18.5 us
  other arithmetic: 28 us -> 20.9 us
    dot_general x18 -> x12, matrix products: 175 us -> 93 us  [matmul(): lax.dot_general(left, right, (dims, ((), ())), preferred_element_type=F32)]
    ppermute x16 -> x17, waiting for transfers between devices: 123 us -> 67.7 us  [shift_y(): return lax.ppermute(x, 'width', [(i, (i + 2) % n) for i in range(n)])]
    ppermute x16, starting transfers between devices: 22 us -> 52.2 us  [shift_core(): return lax.ppermute(x, 'width', [(i, i ^ 1) for i in range(n)])]
    pallas_call x0 -> x2, Pallas kernels: none -> 18.5 us  [matmul_back(): pl.pallas_call(back_kernel, grid=(n // tile,), in_specs=[pl.BlockSpec((m,...]
    squeeze x10, local copies, waits for them, and re-layouts: 13.2 us -> 1.53 us  [reduce_core(): return add(x[:, 0], shift_core(x[:, 1]))]
    add x10, other arithmetic: 11.5 us -> 3.49 us  [add(): return left.astype(F32) + right.astype(F32)]
    ppermute x16 -> x17, starting transfers between devices: 17.5 us -> 16 us  [shift_y(): return lax.ppermute(x, 'width', [(i, (i + 2) % n) for i in range(n)])]
    ppermute x9 -> x8, waiting for transfers between devices: 32.8 us -> 32.6 us  [shift_dp(): return lax.ppermute(x, 'dp', [(i, (i + 1) % n) for i in range(n)])]
  transfers between devices with their start and end apart: 65 -> 65, of which waited for: 32 -> 35; matrix products, arithmetic and copies ran while one was open for 32% -> 15% of each run, Pallas kernels for 0% -> 4%
where the time goes in v2:
time: 452 us; the launch traced here: 446 us
  waiting for transfers between devices  187 us (41%)
  starting transfers between devices  98.4 us (22%)
  matrix products  93 us (21%)
  local copies, waits for them, and re-layouts  26.1 us (6%)
  other arithmetic  20.9 us (5%)
  Pallas kernels  18.5 us (4%)
    dot_general x12, matrix products, matmul(): lax.dot_general(left, right, (dims, ((), ())), preferred_element_type=F32)  93 us
    ppermute x24, waiting for transfers between devices, shift_z(): return lax.ppermute(x, 'hidden', [(i, (i + step) % n) for i in range(n)])  84.8 us
    ppermute x17, waiting for transfers between devices, shift_y(): return lax.ppermute(x, 'width', [(i, (i + 2) % n) for i in range(n)])  67.7 us
    ppermute x16, starting transfers between devices, shift_core(): return lax.ppermute(x, 'width', [(i, i ^ 1) for i in range(n)])  52.2 us
    ppermute x8, waiting for transfers between devices, shift_dp(): return lax.ppermute(x, 'dp', [(i, (i + 1) % n) for i in range(n)])  32.6 us
    ppermute x24, starting transfers between devices, shift_z(): return lax.ppermute(x, 'hidden', [(i, (i + step) % n) for i in range(n)])  24.8 us
    pallas_call x2, Pallas kernels, matmul_back(): pl.pallas_call(back_kernel, grid=(n // tile,), in_specs=[pl.BlockSpec((m,...  18.5 us
    ppermute x17, starting transfers between devices, shift_y(): return lax.ppermute(x, 'width', [(i, (i + 2) % n) for i in range(n)])  16 us
  transfers between devices with their start and end apart: 65, of which 35 were waited for; matrix products, arithmetic and copies ran while one was open for 15% of the time, Pallas kernels for 4%

profile of v2, /device:TPU:1, one launch (start us, length us, event | category | flops | bytes accessed | tf_op | source)
XLA Modules:
  0.0 446.2 jit_solution(4547545915985575048)
XLA Ops:
  11.6 9.1 %convolution_convert_fusion.4 = bf16[256,3584]{1,0:T(8,128)(2,1)S(1)} fusion(bf16[2048,3584]{1,0:T(8,128)(2,1)} %param.9, bf16[512,2048]{1,0:T(8,128)(2,1)S(1)} %convolution_convert_fusion.9), kind=kOutput, calls=%fused_computation.12 | convolution fusion | flops 3759013888 | bytes 17563648 | tf_op jit(solution)/shard_map/dot_general | solution.py:17
  38.0 6.2 %collective-permute-done.2 = bf16[64,3584]{1,0:T(8,128)(2,1)S(1)} collective-permute-done((bf16[64,3584]{1,0:T(8,128)(2,1)S(1)}, bf16[64,3584]{1,0:T(8,128)(2,1)S(1)}, u32[]{:S(2)}, u32[]{:S(2)}) %collective-permute-start.2) | collective-permute-done | bytes 458784 | tf_op jit(solution)/shard_map/ppermute | solution.py:58
  44.3 9.8 %collective-permute-done.4 = bf16[64,3584]{1,0:T(8,128)(2,1)S(1)} collective-permute-done((bf16[64,3584]{1,0:T(8,128)(2,1)S(1)}, bf16[64,3584]{1,0:T(8,128)(2,1)S(1)}, u32[]{:S(2)}, u32[]{:S(2)}) %collective-permute-start.4) | collective-permute-done | bytes 458784 | tf_op jit(solution)/shard_map/ppermute | solution.py:58
  54.1 9.8 %collective-permute-done.6 = bf16[64,3584]{1,0:T(8,128)(2,1)S(1)} collective-permute-done((bf16[64,3584]{1,0:T(8,128)(2,1)S(1)}, bf16[64,3584]{1,0:T(8,128)(2,1)S(1)}, u32[]{:S(2)}, u32[]{:S(2)}) %collective-permute-start.6) | collective-permute-done | bytes 458784 | tf_op jit(solution)/shard_map/ppermute | solution.py:58
  64.6 9.1 %convolution_convert_fusion.2 = bf16[256,3584]{1,0:T(8,128)(2,1)S(1)} fusion(bf16[256,2048]{1,0:T(8,128)(2,1)S(1)} %get-tuple-element.10, bf16[2048,3584]{1,0:T(8,128)(2,1)} %param.8), kind=kOutput, calls=%fused_computation.10 | convolution fusion | flops 3759013888 | bytes 17563648 | tf_op jit(solution)/shard_map/dot_general | solution.py:17
  73.7 9.1 %convolution_convert_fusion.1 = bf16[256,3584]{1,0:T(8,128)(2,1)S(1)} fusion(bf16[256,2048]{1,0:T(8,128)(2,1)S(1)} %get-tuple-element.10, bf16[2048,3584]{1,0:T(8,128)(2,1)} %param.9), kind=kOutput, calls=%fused_computation.9 | convolution fusion | flops 3759013888 | bytes 17563648 | tf_op jit(solution)/shard_map/dot_general | solution.py:17
  86.0 17.8 %collective-permute-done.7 = bf16[2,64,3584]{2,1,0:T(8,128)(2,1)S(1)} collective-permute-done((bf16[2,64,3584]{2,1,0:T(8,128)(2,1)S(1)}, bf16[2,64,3584]{2,1,0:T(8,128)(2,1)S(1)}, u32[]{:S(2)}, u32[]{:S(2)}) %collective-permute-start.7) | collective-permute-done | bytes 917536 | tf_op jit(solution)/shard_map/ppermute | solution.py:58
  106.4 9.7 %convolution_convert_fusion = bf16[256,3584]{1,0:T(8,128)(2,1)S(1)} fusion(bf16[256,2048]{1,0:T(8,128)(2,1)S(1)} %get-tuple-element.10, bf16[2048,3584]{1,0:T(8,128)(2,1)} %param.11), kind=kOutput, calls=%fused_computation.8 | convolution fusion | flops 3759013888 | bytes 17563648 | tf_op jit(solution)/shard_map/dot_general | solution.py:17
  118.8 7.9 %convolution_convert_fusion.7 = bf16[512,2048]{1,0:T(8,128)(2,1)S(1)} fusion(bf16[512,3584]{1,0:T(8,128)(2,1)S(1)} %bitcast.497, bf16[3584,2048]{1,0:T(8,128)(2,1)S(1)} %bitcast.480), kind=kOutput, calls=%fused_computation.21 | convolution fusion | flops 7517241344 | bytes 20447232 | tf_op jit(solution)/shard_map/dot_general | solution.py:17
  151.0 6.2 %collective-permute-done.17 = bf16[4,16,2048]{2,1,0:T(8,128)(2,1)S(1)} collective-permute-done((bf16[4,16,2048]{2,1,0:T(8,128)(2,1)S(1)}, bf16[4,16,2048]{2,1,0:T(8,128)(2,1)S(1)}, u32[]{:S(2)}, u32[]{:S(2)}) %collective-permute-start.17) | collective-permute-done | bytes 262176 | tf_op jit(solution)/shard_map/ppermute | solution.py:63
  160.2 6.2 %collective-permute-done.10 = bf16[4,16,2048]{2,1,0:T(8,128)(2,1)S(1)} collective-permute-done((bf16[4,16,2048]{2,1,0:T(8,128)(2,1)S(1)}, bf16[4,16,2048]{2,1,0:T(8,128)(2,1)S(1)}, u32[]{:S(2)}, u32[]{:S(2)}) %collective-permute-start.10) | collective-permute-done | bytes 262176 | tf_op jit(solution)/shard_map/ppermute | solution.py:63
  175.8 6.6 %collective-permute-done.18 = bf16[4,16,2048]{2,1,0:T(8,128)(2,1)S(1)} collective-permute-done((bf16[4,16,2048]{2,1,0:T(8,128)(2,1)S(1)}, bf16[4,16,2048]{2,1,0:T(8,128)(2,1)S(1)}, u32[]{:S(2)}, u32[]{:S(2)}) %collective-permute-start.18) | collective-permute-done | bytes 262176 | tf_op jit(solution)/shard_map/ppermute | solution.py:63
  185.1 9.5 %collective-permute-done.19 = bf16[4,16,2048]{2,1,0:T(8,128)(2,1)S(1)} collective-permute-done((bf16[4,16,2048]{2,1,0:T(8,128)(2,1)S(1)}, bf16[4,16,2048]{2,1,0:T(8,128)(2,1)S(1)}, u32[]{:S(2)}, u32[]{:S(2)}) %collective-permute-start.19) | collective-permute-done | bytes 262176 | tf_op jit(solution)/shard_map/ppermute | solution.py:63
  196.5 6.3 %collective-permute-start.34 = (bf16[2,2,64,3584]{3,2,0,1:T(8,128)(2,1)S(1)}, bf16[2,2,64,3584]{3,2,0,1:T(8,128)(2,1)S(1)}, u32[]{:S(2)}, u32[]{:S(2)}) collective-permute-start(bf16[2,2,64,3584]{3,2,0,1:T(8,128)(2,1)S(1)} %get-tuple-element.52), channel_id=1, source_target_pairs={{0,4},{4,0},{8,12},{12,8},{1,5},{5,1},{9,13},{13,9},{2,6},{6,2},{1... | collective-permute-start | bytes 5505032 | tf_op jit(solution)/shard_map/ppermute | solution.py:53
  207.5 9.2 %shard_map.77 = bf16[512,3584]{1,0:T(8,128)(2,1)S(1)} custom-call(bf16[512,2048]{1,0:T(8,128)(2,1)S(1)} %pad_maximum_fusion.7.left_ref, bf16[3584,2048]{1,0:T(8,128)(2,1)S(1)} %bitcast.480), custom_call_target="tpu_custom_call" | custom-call | flops 7516192768 | bytes 20447232 | tf_op jit(solution)/shard_map/pallas_call | solution.py:33
  217.6 7.9 %convolution_convert_fusion.6 = bf16[512,2048]{1,0:T(8,128)(2,1)S(1)} fusion(bf16[512,3584]{1,0:T(8,128)(2,1)S(1)} %bitcast.498, bf16[3584,2048]{1,0:T(8,128)(2,1)S(1)} %bitcast.480), kind=kOutput, calls=%fused_computation.20 | convolution fusion | flops 7517241344 | bytes 20447232 | tf_op jit(solution)/shard_map/dot_general | solution.py:17
  233.1 5.8 %collective-permute-start.47 = (bf16[2,64,3584]{2,1,0:T(8,128)(2,1)S(1)}, bf16[2,64,3584]{2,1,0:T(8,128)(2,1)S(1)}, u32[]{:S(2)}, u32[]{:S(2)}) collective-permute-start(bf16[2,64,3584]{2,1,0:T(8,128)(2,1)S(1)} %slice_bitcast_fusion.7), channel_id=1, source_target_pairs={{0,4},{4,0},{8,12},{12,8},{1,5},{5,1},{9,13},{13,9},{2,6},{6,2},{1... | collective-permute-start | bytes 2752520 | tf_op jit(solution)/shard_map/ppermute | solution.py:53
  243.8 6.1 %collective-permute-done.41 = bf16[4,16,2048]{2,1,0:T(8,128)(2,1)S(1)} collective-permute-done((bf16[4,16,2048]{2,1,0:T(8,128)(2,1)S(1)}, bf16[4,16,2048]{2,1,0:T(8,128)(2,1)S(1)}, u32[]{:S(2)}, u32[]{:S(2)}) %collective-permute-start.41) | collective-permute-done | bytes 262176 | tf_op jit(solution)/shard_map/ppermute | solution.py:63
  263.8 6.1 %collective-permute-done.43 = bf16[4,16,2048]{2,1,0:T(8,128)(2,1)S(1)} collective-permute-done((bf16[4,16,2048]{2,1,0:T(8,128)(2,1)S(1)}, bf16[4,16,2048]{2,1,0:T(8,128)(2,1)S(1)}, u32[]{:S(2)}, u32[]{:S(2)}) %collective-permute-start.43) | collective-permute-done | bytes 262176 | tf_op jit(solution)/shard_map/ppermute | solution.py:63
  275.6 7.4 %collective-permute-done.44 = bf16[4,16,2048]{2,1,0:T(8,128)(2,1)} collective-permute-done((bf16[4,16,2048]{2,1,0:T(8,128)(2,1)}, bf16[4,16,2048]{2,1,0:T(8,128)(2,1)}, u32[]{:S(2)}, u32[]{:S(2)}) %collective-permute-start.44) | collective-permute-done | bytes 262176 | tf_op jit(solution)/shard_map/ppermute | solution.py:63
  301.8 5.2 %copy-done.2 = bf16[3584,2048]{1,0:T(8,128)(2,1)S(1)} copy-done((bf16[3584,2048]{1,0:T(8,128)(2,1)S(1)}, bf16[3584,2048]{1,0:T(8,128)(2,1)}, u32[]{:S(2)}) %copy-start.2) | copy-done | bytes 14680088
  307.0 9.2 %shard_map.78 = bf16[512,3584]{1,0:T(8,128)(2,1)S(1)} custom-call(bf16[512,2048]{1,0:T(8,128)(2,1)S(1)} %pad_maximum_fusion.8.left_ref, bf16[3584,2048]{1,0:T(8,128)(2,1)S(1)} %copy-done.2), custom_call_target="tpu_custom_call" | custom-call | flops 7516192768 | bytes 20447232 | tf_op jit(solution)/shard_map/pallas_call | solution.py:33
  316.6 14.8 %collective-permute-start.49 = (bf16[2,64,3584]{2,1,0:T(8,128)(2,1)S(1)}, bf16[2,64,3584]{2,1,0:T(8,128)(2,1)S(1)}, u32[]{:S(2)}, u32[]{:S(2)}) collective-permute-start(bf16[2,64,3584]{2,1,0:T(8,128)(2,1)S(1)} %slice_bitcast_fusion.4), channel_id=1, source_target_pairs={{0,4},{4,0},{8,12},{12,8},{1,5},{5,1},{9,13},{13,9},{2,6},{6,2},{1... | collective-permute-start | bytes 2752520 | tf_op jit(solution)/shard_map/ppermute | solution.py:53
  336.4 19.6 %collective-permute-done.57 = bf16[64,3584]{1,0:T(8,128)(2,1)S(1)} collective-permute-done((bf16[64,3584]{1,0:T(8,128)(2,1)S(1)}, bf16[64,3584]{1,0:T(8,128)(2,1)S(1)}, u32[]{:S(2)}, u32[]{:S(2)}) %collective-permute-start.57) | collective-permute-done | bytes 458784 | tf_op jit(solution)/shard_map/ppermute | solution.py:68
  358.3 8.2 %collective-permute-done.60 = bf16[64,3584]{1,0:T(8,128)(2,1)S(1)} collective-permute-done((bf16[64,3584]{1,0:T(8,128)(2,1)S(1)}, bf16[64,3584]{1,0:T(8,128)(2,1)S(1)}, u32[]{:S(2)}, u32[]{:S(2)}) %collective-permute-start.60) | collective-permute-done | bytes 458784 | tf_op jit(solution)/shard_map/ppermute | solution.py:58
  370.0 7.2 %collective-permute-done.62 = bf16[64,3584]{1,0:T(8,128)(2,1)S(1)} collective-permute-done((bf16[64,3584]{1,0:T(8,128)(2,1)S(1)}, bf16[64,3584]{1,0:T(8,128)(2,1)S(1)}, u32[]{:S(2)}, u32[]{:S(2)}) %collective-permute-start.62) | collective-permute-done | bytes 458784 | tf_op jit(solution)/shard_map/ppermute | solution.py:68
  378.3 5.9 %collective-permute-start.26 = (bf16[4,64,3584]{2,1,0:T(8,128)(2,1)S(1)}, bf16[4,64,3584]{2,1,0:T(8,128)(2,1)S(1)}, u32[]{:S(2)}, u32[]{:S(2)}) collective-permute-start(bf16[4,64,3584]{2,1,0:T(8,128)(2,1)S(1)} %get-tuple-element.46), channel_id=1, source_target_pairs={{0,4},{4,0},{8,12},{12,8},{1,5},{5,1},{9,13},{13,9},{2,6},{6,2},{1... | collective-permute-start | bytes 5505032 | tf_op jit(solution)/shard_map/ppermute | solution.py:53
  388.5 9.5 %collective-permute-done.63 = bf16[64,3584]{1,0:T(8,128)(2,1)S(1)} collective-permute-done((bf16[64,3584]{1,0:T(8,128)(2,1)S(1)}, bf16[64,3584]{1,0:T(8,128)(2,1)S(1)}, u32[]{:S(2)}, u32[]{:S(2)}) %collective-permute-start.63) | collective-permute-done | bytes 458784 | tf_op jit(solution)/shard_map/ppermute | solution.py:58
  398.6 5.4 %collective-permute-start.64 = (bf16[4,64,3584]{2,1,0:T(8,128)(2,1)S(1)}, bf16[4,64,3584]{2,1,0:T(8,128)(2,1)S(1)}, u32[]{:S(2)}, u32[]{:S(2)}) collective-permute-start(bf16[4,64,3584]{2,1,0:T(8,128)(2,1)S(1)} %get-tuple-element.44), channel_id=1, source_target_pairs={{0,4},{4,0},{8,12},{12,8},{1,5},{5,1},{9,13},{13,9},{2,6},{6,2},{1... | collective-permute-start | bytes 5505032 | tf_op jit(solution)/shard_map/ppermute | solution.py:53
  404.0 5.8 %collective-permute-done.53 = bf16[64,3584]{1,0:T(8,128)(2,1)S(1)} collective-permute-done((bf16[64,3584]{1,0:T(8,128)(2,1)S(1)}, bf16[64,3584]{1,0:T(8,128)(2,1)S(1)}, u32[]{:S(2)}, u32[]{:S(2)}) %collective-permute-start.53) | collective-permute-done | bytes 458784 | tf_op jit(solution)/shard_map/ppermute | solution.py:68
  420.1 14.2 %multiply_convert_fusion = bf16[1024,3584]{1,0:T(8,128)(2,1)} fusion(bf16[512,3584]{1,0:T(8,128)(2,1)} %bitcast.495, bf16[512,3584]{1,0:T(8,128)(2,1)S(1)} %bitcast.493, bf16[2048,3584]{1,0:T(8,128)(2,1)} %param.11, s32[]{:T(128)S(6)} %select_n.75, bf16[256,1024]{1,0:T(8,128)(2,1)S(1)} %get-tuple-element.54, bf16[256,1024]{1,0:T(8,128)(2,1)S(1)} %get-tuple-element.28, ...), kind=kOutput, calls=%fused_computation | convolution fusion | flops 7557611520 | bytes 24117252 | tf_op jit(solution)/shard_map/dot_general | solution.py:17
  434.4 11.6 %multiply_convert_fusion.1 = bf16[1024,3584]{1,0:T(8,128)(2,1)} fusion(bf16[512,3584]{1,0:T(8,128)(2,1)} %bitcast.496, bf16[512,3584]{1,0:T(8,128)(2,1)S(1)} %bitcast.494, bf16[256,1024]{1,0:T(8,128)(2,1)S(1)} %get-tuple-element.54, bf16[256,1024]{1,0:T(8,128)(2,1)S(1)} %get-tuple-element.28, bf16[256,1024]{1,0:T(8,128)(2,1)S(1)} %get-tuple-element.53, ...), kind=kOutput, calls=%fused_computation.1 | convolution fusion | flops 7546601472 | bytes 16777216 | tf_op jit(solution)/shard_map/dot_general | solution.py:17
  (266 shorter events, 161.7 us)
Async XLA Ops:
  11.5 14.2 %collective-permute-start.1 = (bf16[2,64,3584]{2,1,0:T(8,128)(2,1)S(1)}, bf16[2,64,3584]{2,1,0:T(8,128)(2,1)S(1)}, u32[]{:S(2)}, u32[]{:S(2)}) collective-permute-start(bf16[2,64,3584]{2,1,0:T(8,128)(2,1)S(1)} %slice_bitcast_fusion.28), channel_id=1, source_target_pairs={{0,4},{4,0},{8,12},{12,8},{1,5},{5,1},{9,13},{13,9},{2,6},{6,2},{1... | collective-permute-start | bytes 2752520 | tf_op jit(solution)/shard_map/ppermute | solution.py:53
  34.1 20.0 %collective-permute-start.4 = (bf16[64,3584]{1,0:T(8,128)(2,1)S(1)}, bf16[64,3584]{1,0:T(8,128)(2,1)S(1)}, u32[]{:S(2)}, u32[]{:S(2)}) collective-permute-start(bf16[64,3584]{1,0:T(8,128)(2,1)S(1)} %fusion.67), channel_id=1, source_target_pairs={{0,8},{4,12},{8,0},{12,4},{1,9},{5,13},{9,1},{13,5},{2,10},{6,14},... | collective-permute-start | bytes 1376264 | tf_op jit(solution)/shard_map/ppermute | solution.py:58
  34.5 29.4 %collective-permute-start.6 = (bf16[64,3584]{1,0:T(8,128)(2,1)S(1)}, bf16[64,3584]{1,0:T(8,128)(2,1)S(1)}, u32[]{:S(2)}, u32[]{:S(2)}) collective-permute-start(bf16[64,3584]{1,0:T(8,128)(2,1)S(1)} %fusion.68), channel_id=1, source_target_pairs={{0,8},{4,12},{8,0},{12,4},{1,9},{5,13},{9,1},{13,5},{2,10},{6,14},... | collective-permute-start | bytes 1376264 | tf_op jit(solution)/shard_map/ppermute | solution.py:58
  82.9 20.9 %collective-permute-start.7 = (bf16[2,64,3584]{2,1,0:T(8,128)(2,1)S(1)}, bf16[2,64,3584]{2,1,0:T(8,128)(2,1)S(1)}, u32[]{:S(2)}, u32[]{:S(2)}) collective-permute-start(bf16[2,64,3584]{2,1,0:T(8,128)(2,1)S(1)} %get-tuple-element.56), channel_id=1, source_target_pairs={{0,8},{4,12},{8,0},{12,4},{1,9},{5,13},{9,1},{13,5},{2,10},{6,14},... | collective-permute-start | bytes 2752520 | tf_op jit(solution)/shard_map/ppermute | solution.py:58
  84.2 21.9 %collective-permute-start.27 = (bf16[2,64,3584]{2,1,0:T(8,128)(2,1)S(1)}, bf16[2,64,3584]{2,1,0:T(8,128)(2,1)S(1)}, u32[]{:S(2)}, u32[]{:S(2)}) collective-permute-start(bf16[2,64,3584]{2,1,0:T(8,128)(2,1)S(1)} %slice_bitcast_fusion.16), channel_id=1, source_target_pairs={{0,4},{4,0},{8,12},{12,8},{1,5},{5,1},{9,13},{13,9},{2,6},{6,2},{1... | collective-permute-start | bytes 2752520 | tf_op jit(solution)/shard_map/ppermute | solution.py:53
  86.0 32.0 %collective-permute-start.29 = (bf16[2,64,3584]{2,1,0:T(8,128)(2,1)S(1)}, bf16[2,64,3584]{2,1,0:T(8,128)(2,1)S(1)}, u32[]{:S(2)}, u32[]{:S(2)}) collective-permute-start(bf16[2,64,3584]{2,1,0:T(8,128)(2,1)S(1)} %slice_bitcast_fusion.13), channel_id=1, source_target_pairs={{0,4},{4,0},{8,12},{12,8},{1,5},{5,1},{9,13},{13,9},{2,6},{6,2},{1... | collective-permute-start | bytes 2752520 | tf_op jit(solution)/shard_map/ppermute | solution.py:53
  104.1 14.1 %collective-permute-start.8 = (bf16[2,2,64,3584]{3,2,1,0:T(8,128)(2,1)S(1)}, bf16[2,2,64,3584]{3,2,1,0:T(8,128)(2,1)S(1)}, u32[]{:S(2)}, u32[]{:S(2)}) collective-permute-start(bf16[2,2,64,3584]{3,2,1,0:T(8,128)(2,1)S(1)} %get-tuple-element.50), channel_id=1, source_target_pairs={{0,4},{4,0},{8,12},{12,8},{1,5},{5,1},{9,13},{13,9},{2,6},{6,2},{1... | collective-permute-start | bytes 5505032 | tf_op jit(solution)/shard_map/ppermute | solution.py:53
  117.0 22.5 %collective-permute-start.31 = (bf16[2,64,3584]{2,1,0:T(8,128)(2,1)}, bf16[2,64,3584]{2,1,0:T(8,128)(2,1)}, u32[]{:S(2)}, u32[]{:S(2)}) collective-permute-start(bf16[2,64,3584]{2,1,0:T(8,128)(2,1)} %slice_bitcast_fusion.10), channel_id=1, source_target_pairs={{0,4},{4,0},{8,12},{12,8},{1,5},{5,1},{9,13},{13,9},{2,6},{6,2},{1... | collective-permute-start | bytes 2752520 | tf_op jit(solution)/shard_map/ppermute | solution.py:53
  130.1 27.5 %collective-permute-start.30 = (bf16[64,3584]{1,0:T(8,128)(2,1)S(1)}, bf16[64,3584]{1,0:T(8,128)(2,1)S(1)}, u32[]{:S(2)}, u32[]{:S(2)}) collective-permute-start(bf16[64,3584]{1,0:T(8,128)(2,1)S(1)} %fusion.71), channel_id=1, source_target_pairs={{0,8},{4,12},{8,0},{12,4},{1,9},{5,13},{9,1},{13,5},{2,10},{6,14},... | collective-permute-start | bytes 1376264 | tf_op jit(solution)/shard_map/ppermute | solution.py:58
  131.4 26.2 %collective-permute-start.28 = (bf16[64,3584]{1,0:T(8,128)(2,1)S(1)}, bf16[64,3584]{1,0:T(8,128)(2,1)S(1)}, u32[]{:S(2)}, u32[]{:S(2)}) collective-permute-start(bf16[64,3584]{1,0:T(8,128)(2,1)S(1)} %copy-done.21), channel_id=1, source_target_pairs={{0,8},{4,12},{8,0},{12,4},{1,9},{5,13},{9,1},{13,5},{2,10},{6,14},... | collective-permute-start | bytes 1376264 | tf_op jit(solution)/shard_map/ppermute | solution.py:58
  166.7 29.6 %collective-permute-start.33 = (bf16[2,64,3584]{2,1,0:T(8,128)(2,1)S(1)}, bf16[2,64,3584]{2,1,0:T(8,128)(2,1)S(1)}, u32[]{:S(2)}, u32[]{:S(2)}) collective-permute-start(bf16[2,64,3584]{2,1,0:T(8,128)(2,1)S(1)} %get-tuple-element.58), channel_id=1, source_target_pairs={{0,8},{4,12},{8,0},{12,4},{1,9},{5,13},{9,1},{13,5},{2,10},{6,14},... | collective-permute-start | bytes 2752520 | tf_op jit(solution)/shard_map/ppermute | solution.py:58
  168.0 14.4 %collective-permute-start.18 = (bf16[4,16,2048]{2,1,0:T(8,128)(2,1)S(1)}, bf16[4,16,2048]{2,1,0:T(8,128)(2,1)S(1)}, u32[]{:S(2)}, u32[]{:S(2)}) collective-permute-start(bf16[4,16,2048]{2,1,0:T(8,128)(2,1)S(1)} %get-tuple-element.35), channel_id=1, source_target_pairs={{0,3},{1,0},{2,1},{3,2},{4,7},{5,4},{6,5},{7,6},{8,11},{9,8},{10,9... | collective-permute-start | bytes 786440 | tf_op jit(solution)/shard_map/ppermute | solution.py:63
  196.5 20.5 %collective-permute-start.34 = (bf16[2,2,64,3584]{3,2,0,1:T(8,128)(2,1)S(1)}, bf16[2,2,64,3584]{3,2,0,1:T(8,128)(2,1)S(1)}, u32[]{:S(2)}, u32[]{:S(2)}) collective-permute-start(bf16[2,2,64,3584]{3,2,0,1:T(8,128)(2,1)S(1)} %get-tuple-element.52), channel_id=1, source_target_pairs={{0,4},{4,0},{8,12},{12,8},{1,5},{5,1},{9,13},{13,9},{2,6},{6,2},{1... | collective-permute-start | bytes 5505032 | tf_op jit(solution)/shard_map/ppermute | solution.py:53
  226.0 16.5 %collective-permute-start.21 = (bf16[2,64,3584]{2,1,0:T(8,128)(2,1)S(1)}, bf16[2,64,3584]{2,1,0:T(8,128)(2,1)S(1)}, u32[]{:S(2)}, u32[]{:S(2)}) collective-permute-start(bf16[2,64,3584]{2,1,0:T(8,128)(2,1)S(1)} %slice_bitcast_fusion.19), channel_id=1, source_target_pairs={{0,4},{4,0},{8,12},{12,8},{1,5},{5,1},{9,13},{13,9},{2,6},{6,2},{1... | collective-permute-start | bytes 2752520 | tf_op jit(solution)/shard_map/ppermute | solution.py:53
  233.1 22.7 %collective-permute-start.47 = (bf16[2,64,3584]{2,1,0:T(8,128)(2,1)S(1)}, bf16[2,64,3584]{2,1,0:T(8,128)(2,1)S(1)}, u32[]{:S(2)}, u32[]{:S(2)}) collective-permute-start(bf16[2,64,3584]{2,1,0:T(8,128)(2,1)S(1)} %slice_bitcast_fusion.7), channel_id=1, source_target_pairs={{0,4},{4,0},{8,12},{12,8},{1,5},{5,1},{9,13},{13,9},{2,6},{6,2},{1... | collective-permute-start | bytes 2752520 | tf_op jit(solution)/shard_map/ppermute | solution.py:53
  243.7 39.3 %collective-permute-start.22 = (bf16[64,3584]{1,0:T(8,128)(2,1)}, bf16[64,3584]{1,0:T(8,128)(2,1)}, u32[]{:S(2)}, u32[]{:S(2)}) collective-permute-start(bf16[64,3584]{1,0:T(8,128)(2,1)} %fusion.69), channel_id=1, source_target_pairs={{0,8},{4,12},{8,0},{12,4},{1,9},{5,13},{9,1},{13,5},{2,10},{6,14},... | collective-permute-start | bytes 1376264 | tf_op jit(solution)/shard_map/ppermute | solution.py:58
  263.7 19.2 %collective-permute-start.48 = (bf16[64,3584]{1,0:T(8,128)(2,1)}, bf16[64,3584]{1,0:T(8,128)(2,1)}, u32[]{:S(2)}, u32[]{:S(2)}) collective-permute-start(bf16[64,3584]{1,0:T(8,128)(2,1)} %fusion.73), channel_id=1, source_target_pairs={{0,8},{4,12},{8,0},{12,4},{1,9},{5,13},{9,1},{13,5},{2,10},{6,14},... | collective-permute-start | bytes 1376264 | tf_op jit(solution)/shard_map/ppermute | solution.py:58
  273.1 139.7 %collective-permute-start = (bf16[512,1024]{1,0:T(8,128)(2,1)}, bf16[512,1024]{1,0:T(8,128)(2,1)}, u32[]{:S(2)}, u32[]{:S(2)}) collective-permute-start(bf16[512,1024]{1,0:T(8,128)(2,1)} %constant_dynamic-slice_fusion.1), channel_id=1, source_target_pairs={{0,16},{16,0},{1,17},{17,1},{2,18},{18,2},{3,19},{19,3},{4,20},{20... | collective-permute-start | bytes 3145736 | tf_op jit(solution)/shard_map/ppermute | solution.py:68
  274.3 15.1 %collective-permute-start.39 = (bf16[4,16,2048]{2,1,0:T(8,128)(2,1)}, bf16[4,16,2048]{2,1,0:T(8,128)(2,1)S(1)}, u32[]{:S(2)}, u32[]{:S(2)}) collective-permute-start(bf16[4,16,2048]{2,1,0:T(8,128)(2,1)} %collective-permute-done.38), channel_id=1, source_target_pairs={{0,1},{1,2},{2,3},{3,0},{4,5},{5,6},{6,7},{7,4},{8,9},{9,10},{10,1... | collective-permute-start | bytes 786440 | tf_op jit(solution)/shard_map/ppermute | solution.py:63
  286.3 47.8 %collective-permute-start.55 = (bf16[64,3584]{1,0:T(8,128)(2,1)S(1)}, bf16[64,3584]{1,0:T(8,128)(2,1)S(1)}, u32[]{:S(2)}, u32[]{:S(2)}) collective-permute-start(bf16[64,3584]{1,0:T(8,128)(2,1)S(1)} %get-tuple-element.16), channel_id=1, source_target_pairs={{0,8},{4,12},{8,0},{12,4},{1,9},{5,13},{9,1},{13,5},{2,10},{6,14},... | collective-permute-start | bytes 1376264 | tf_op jit(solution)/shard_map/ppermute | solution.py:58
  288.1 48.1 %collective-permute-start.56 = (bf16[64,3584]{1,0:T(8,128)(2,1)S(1)}, bf16[64,3584]{1,0:T(8,128)(2,1)S(1)}, u32[]{:S(2)}, u32[]{:S(2)}) collective-permute-start(bf16[64,3584]{1,0:T(8,128)(2,1)S(1)} %get-tuple-element.16), channel_id=1, source_target_pairs={{0,16},{16,0},{1,17},{17,1},{2,18},{18,2},{3,19},{19,3},{4,20},{20... | collective-permute-start | bytes 1376264 | tf_op jit(solution)/shard_map/ppermute | solution.py:68
  296.5 37.7 %collective-permute-start.23 = (bf16[64,3584]{1,0:T(8,128)(2,1)S(1)}, bf16[64,3584]{1,0:T(8,128)(2,1)S(1)}, u32[]{:S(2)}, u32[]{:S(2)}) collective-permute-start(bf16[64,3584]{1,0:T(8,128)(2,1)S(1)} %fusion.23), channel_id=1, source_target_pairs={{0,8},{4,12},{8,0},{12,4},{1,9},{5,13},{9,1},{13,5},{2,10},{6,14},... | collective-permute-start | bytes 1376264 | tf_op jit(solution)/shard_map/ppermute | solution.py:58
  316.6 16.9 %collective-permute-start.49 = (bf16[2,64,3584]{2,1,0:T(8,128)(2,1)S(1)}, bf16[2,64,3584]{2,1,0:T(8,128)(2,1)S(1)}, u32[]{:S(2)}, u32[]{:S(2)}) collective-permute-start(bf16[2,64,3584]{2,1,0:T(8,128)(2,1)S(1)} %slice_bitcast_fusion.4), channel_id=1, source_target_pairs={{0,4},{4,0},{8,12},{12,8},{1,5},{5,1},{9,13},{13,9},{2,6},{6,2},{1... | collective-permute-start | bytes 2752520 | tf_op jit(solution)/shard_map/ppermute | solution.py:53
  334.1 34.4 %collective-permute-start.24 = (bf16[64,3584]{1,0:T(8,128)(2,1)S(1)}, bf16[64,3584]{1,0:T(8,128)(2,1)S(1)}, u32[]{:S(2)}, u32[]{:S(2)}) collective-permute-start(bf16[64,3584]{1,0:T(8,128)(2,1)S(1)} %fusion.23), channel_id=1, source_target_pairs={{0,16},{16,0},{1,17},{17,1},{2,18},{18,2},{3,19},{19,3},{4,20},{20... | collective-permute-start | bytes 1376264 | tf_op jit(solution)/shard_map/ppermute | solution.py:68
  334.2 21.8 %collective-permute-start.57 = (bf16[64,3584]{1,0:T(8,128)(2,1)S(1)}, bf16[64,3584]{1,0:T(8,128)(2,1)S(1)}, u32[]{:S(2)}, u32[]{:S(2)}) collective-permute-start(bf16[64,3584]{1,0:T(8,128)(2,1)S(1)} %collective-permute-done.55), channel_id=1, source_target_pairs={{0,16},{16,0},{1,17},{17,1},{2,18},{18,2},{3,19},{19,3},{4,20},{20... | collective-permute-start | bytes 1376264 | tf_op jit(solution)/shard_map/ppermute | solution.py:68
  335.9 32.7 %collective-permute-start.25 = (bf16[64,3584]{1,0:T(8,128)(2,1)S(1)}, bf16[64,3584]{1,0:T(8,128)(2,1)S(1)}, u32[]{:S(2)}, u32[]{:S(2)}) collective-permute-start(bf16[64,3584]{1,0:T(8,128)(2,1)S(1)} %collective-permute-done.23), channel_id=1, source_target_pairs={{0,16},{16,0},{1,17},{17,1},{2,18},{18,2},{3,19},{19,3},{4,20},{20... | collective-permute-start | bytes 1376264 | tf_op jit(solution)/shard_map/ppermute | solution.py:68
  336.2 20.2 %collective-permute-start.50 = (bf16[64,3584]{1,0:T(8,128)(2,1)S(1)}, bf16[64,3584]{1,0:T(8,128)(2,1)S(1)}, u32[]{:S(2)}, u32[]{:S(2)}) collective-permute-start(bf16[64,3584]{1,0:T(8,128)(2,1)S(1)} %fusion.74), channel_id=1, source_target_pairs={{0,8},{4,12},{8,0},{12,4},{1,9},{5,13},{9,1},{13,5},{2,10},{6,14},... | collective-permute-start | bytes 1376264 | tf_op jit(solution)/shard_map/ppermute | solution.py:58
  356.5 57.6 %collective-permute-start.58 = (bf16[4,64,3584]{2,1,0:T(8,128)(2,1)S(1)}, bf16[4,64,3584]{2,1,0:T(8,128)(2,1)S(1)}, u32[]{:S(2)}, u32[]{:S(2)}) collective-permute-start(bf16[4,64,3584]{2,1,0:T(8,128)(2,1)S(1)} %get-tuple-element.42), channel_id=1, source_target_pairs={{0,4},{4,0},{8,12},{12,8},{1,5},{5,1},{9,13},{13,9},{2,6},{6,2},{1... | collective-permute-start | bytes 5505032 | tf_op jit(solution)/shard_map/ppermute | solution.py:53
  368.6 19.5 %collective-permute-start.51 = (bf16[64,3584]{1,0:T(8,128)(2,1)S(1)}, bf16[64,3584]{1,0:T(8,128)(2,1)S(1)}, u32[]{:S(2)}, u32[]{:S(2)}) collective-permute-start(bf16[64,3584]{1,0:T(8,128)(2,1)S(1)} %fusion.26), channel_id=1, source_target_pairs={{0,8},{4,12},{8,0},{12,4},{1,9},{5,13},{9,1},{13,5},{2,10},{6,14},... | collective-permute-start | bytes 1376264 | tf_op jit(solution)/shard_map/ppermute | solution.py:58
  377.2 20.8 %collective-permute-start.63 = (bf16[64,3584]{1,0:T(8,128)(2,1)S(1)}, bf16[64,3584]{1,0:T(8,128)(2,1)S(1)}, u32[]{:S(2)}, u32[]{:S(2)}) collective-permute-start(bf16[64,3584]{1,0:T(8,128)(2,1)S(1)} %collective-permute-done.62), channel_id=1, source_target_pairs={{0,8},{4,12},{8,0},{12,4},{1,9},{5,13},{9,1},{13,5},{2,10},{6,14},... | collective-permute-start | bytes 1376264 | tf_op jit(solution)/shard_map/ppermute | solution.py:58
  378.3 36.3 %collective-permute-start.26 = (bf16[4,64,3584]{2,1,0:T(8,128)(2,1)S(1)}, bf16[4,64,3584]{2,1,0:T(8,128)(2,1)S(1)}, u32[]{:S(2)}, u32[]{:S(2)}) collective-permute-start(bf16[4,64,3584]{2,1,0:T(8,128)(2,1)S(1)} %get-tuple-element.46), channel_id=1, source_target_pairs={{0,4},{4,0},{8,12},{12,8},{1,5},{5,1},{9,13},{13,9},{2,6},{6,2},{1... | collective-permute-start | bytes 5505032 | tf_op jit(solution)/shard_map/ppermute | solution.py:53
  398.6 16.6 %collective-permute-start.64 = (bf16[4,64,3584]{2,1,0:T(8,128)(2,1)S(1)}, bf16[4,64,3584]{2,1,0:T(8,128)(2,1)S(1)}, u32[]{:S(2)}, u32[]{:S(2)}) collective-permute-start(bf16[4,64,3584]{2,1,0:T(8,128)(2,1)S(1)} %get-tuple-element.44), channel_id=1, source_target_pairs={{0,4},{4,0},{8,12},{12,8},{1,5},{5,1},{9,13},{13,9},{2,6},{6,2},{1... | collective-permute-start | bytes 5505032 | tf_op jit(solution)/shard_map/ppermute | solution.py:53
  (65 other events, 665.0 us)
